TPU v7x, 256 devices: a whole 4x4x8 slice. The times are simulated.
256 devices in a mesh: grp: 16 (over z_lo, x), dev: 16 (over y, z_hi, core).
Axes of the slice: x: 4, y: 4, z: 8 (z_hi: 2, z_lo: 4; z = z_hi * 4 + z_lo), core: 2. Of those that a mesh axis runs over, the one named last changes fastest.
Arguments:
- teacher_image: bfloat16 [16384, 1280], P(('grp', 'dev')), may hold values from -4 to 4
- teacher_text: bfloat16 [16384, 1280], P(('grp', 'dev')), may hold values from -4 to 4
- student_image: bfloat16 [16384, 512], P(('grp', 'dev')), may hold values from -4 to 4
- student_text: bfloat16 [16384, 512], P(('grp', 'dev')), may hold values from -4 to 4
- teacher_scale: float32 [1], replicated, may hold values from 2 to 4
- student_scale: float32 [1], replicated, may hold values from 2 to 4
Outputs:
- grad_image: float32 [16384, 512], P(('grp', 'dev'))
- grad_text: float32 [16384, 512], P(('grp', 'dev'))
- loss: float32 [1], replicated
- grad_scale: float32 [1], replicated
All inputs are finite; a program needn't handle non-finite values.
Results may differ from a plain program's by a relative error of at most 0.0028.
Values may be sent and summed in bfloat16 or wider, within the bound.
A program may use at most 64 MiB of HBM per device.

v0:
```python
import jax
import jax.numpy as jnp
from jax import lax
from jax.sharding import PartitionSpec as P


def exp_total(values, peak, dim):
    return jnp.sum(jnp.exp(values - jnp.expand_dims(peak, dim)), axis=dim)


def lse_grp(teacher, student, dim):
    tpeak, speak = lax.pmax((jnp.max(teacher, axis=dim), jnp.max(student, axis=dim)), "grp")
    ttotal, stotal = lax.psum(
        (exp_total(teacher, tpeak, dim), exp_total(student, speak, dim)), "grp"
    )
    return (tpeak + jnp.log(ttotal), speak + jnp.log(stotal))


def lse_dev(teacher, student, dim):
    tpeak, speak = lax.pmax((jnp.max(teacher, axis=dim), jnp.max(student, axis=dim)), "dev")
    ttotal, stotal = lax.psum(
        (exp_total(teacher, tpeak, dim), exp_total(student, speak, dim)), "dev"
    )
    return (tpeak + jnp.log(ttotal), speak + jnp.log(stotal))


def gather_grp(teacher_rows, student_rows):
    return (
        lax.all_gather(teacher_rows, "grp", axis=0, tiled=True),
        lax.all_gather(student_rows, "grp", axis=0, tiled=True),
    )


def gather_dev(teacher_rows, student_rows):
    return (
        lax.all_gather(teacher_rows, "dev", axis=0, tiled=True),
        lax.all_gather(student_rows, "dev", axis=0, tiled=True),
    )


def back_grp(terms, rows):
    return lax.psum_scatter(
        terms(jnp.int32(0), rows * lax.axis_size("grp")), "grp", scatter_dimension=0, tiled=True
    )


def back_dev(terms, rows):
    return lax.psum_scatter(
        terms(jnp.int32(0), rows * lax.axis_size("dev")), "dev", scatter_dimension=0, tiled=True
    )


def pair_dot(left, right):
    return lax.dot_general(
        left, right, (((1,), (1,)), ((), ())), preferred_element_type=jnp.float32
    )


def finish(
    own_rows,
    image_t,
    image_s,
    text_t,
    text_s,
    teach_scale,
    learn_scale,
    row_lse,
    col_lse,
    image_back,
    text_back,
):
    image_count = image_t.shape[0] // own_rows
    text_count = text_t.shape[0] // own_rows
    pairs_all = own_rows * image_count * text_count
    teacher = teach_scale * pair_dot(image_t, text_t)
    student = learn_scale * pair_dot(image_s, text_s)
    row_teach, row_stud = row_lse(teacher, student, 1)
    col_teach, col_stud = col_lse(teacher, student, 0)
    p_teach = jnp.exp(teacher - row_teach[:, None])
    q_teach = jnp.exp(teacher - col_teach[None, :])
    p_stud = jnp.exp(student - row_stud[:, None])
    q_stud = jnp.exp(student - col_stud[None, :])
    differ = p_stud + q_stud - p_teach - q_teach
    weights = (0.5 * learn_scale * differ).astype(jnp.bfloat16)

    def image_terms(start, count):
        return jnp.dot(weights, text_s, preferred_element_type=jnp.float32)

    def text_terms(start, count):
        return lax.dot_general(
            weights, image_s, (((0,), (0,)), ((), ())), preferred_element_type=jnp.float32
        )

    grad_image = image_back(image_terms, own_rows)
    grad_text = text_back(text_terms, own_rows)
    loss_part = (
        jnp.sum(row_stud) / image_count
        + jnp.sum(col_stud) / text_count
        - jnp.sum((p_teach + q_teach) * student)
    )
    scale_part = jnp.sum(differ * student)
    loss_total, scale_total = lax.psum((loss_part, scale_part), ("grp", "dev"))
    loss = loss_total / (2.0 * pairs_all)
    grad_scale = scale_total / (2.0 * pairs_all * learn_scale)
    return (grad_image, grad_text, loss.reshape(1), grad_scale.reshape(1))


def shards(teacher_image, teacher_text, student_image, student_text, teacher_scale, student_scale):
    own_rows = teacher_image.shape[0]
    teach_scale = teacher_scale[0]
    learn_scale = student_scale[0]
    image_t, image_s = gather_grp(teacher_image, student_image)
    text_t, text_s = gather_dev(teacher_text, student_text)
    return finish(
        own_rows,
        image_t,
        image_s,
        text_t,
        text_s,
        teach_scale,
        learn_scale,
        lse_grp,
        lse_dev,
        back_grp,
        back_dev,
    )


def solution(mesh):
    return jax.shard_map(
        shards,
        mesh=mesh,
        in_specs=(
            P(("grp", "dev"), None),
            P(("grp", "dev"), None),
            P(("grp", "dev"), None),
            P(("grp", "dev"), None),
            P(),
            P(),
        ),
        out_specs=(P(("grp", "dev"), None), P(("grp", "dev"), None), P(), P()),
        check_vma=False,
    )
```

profile of v0, /device:TPU:1, one launch (start us, length us, event | category | flops | bytes accessed | tf_op | source)
XLA Modules:
  0.0 664.2 jit_solution(14882136313879509058)
XLA Ops:
  7.2 0.0 all-gather.5.cloned.1.call-start
  7.2 0.7 all-gather.5.cloned.1.call-update
  7.9 0.0 all-gather.7.cloned.1.call-start
  7.9 0.7 all-gather.7.cloned.1.call-update
  8.6 0.0 all-gather.9.cloned.1.call-start
  8.7 0.7 all-gather.9.cloned.1.call-update
  9.4 0.0 all-gather.11.cloned.1.call-start
  9.4 0.5 all-gather.11.cloned.1.call-update
  10.0 0.0 reduce-scatter.5.cloned.1.call-start
  11.3 73.1 %all-gather.5.cloned.1.call-done = bf16[1024,512]{1,0:T(8,128)(2,1)} async-done(((bf16[64,512]{1,0:T(8,128)(2,1)}), bf16[1024,512]{1,0:T(8,128)(2,1)}) %all-gather.5.cloned.1.call-update) | async-done | bytes 1048592 | tf_op jit(solution)/shard_map/all_gather | solution.py:30
  84.4 67.4 %all-gather.7.cloned.1.call-done = bf16[1024,512]{1,0:T(8,128)(2,1)} async-done(((bf16[64,512]{1,0:T(8,128)(2,1)}), bf16[1024,512]{1,0:T(8,128)(2,1)}) %all-gather.7.cloned.1.call-update) | async-done | bytes 1048592 | tf_op jit(solution)/shard_map/all_gather | solution.py:37
  151.7 4.7 multiply_reduce_fusion.5
  156.5 67.3 %all-gather.9.cloned.1.call-done = bf16[1024,1280]{1,0:T(8,128)(2,1)} async-done(((bf16[64,1280]{1,0:T(8,128)(2,1)}), bf16[1024,1280]{1,0:T(8,128)(2,1)}) %all-gather.9.cloned.1.call-update) | async-done | bytes 2621456 | tf_op jit(solution)/shard_map/all_gather | solution.py:29
  223.8 77.8 %all-gather.11.cloned.1.call-done = bf16[1024,1280]{1,0:T(8,128)(2,1)} async-done(((bf16[64,1280]{1,0:T(8,128)(2,1)}), bf16[1024,1280]{1,0:T(8,128)(2,1)}) %all-gather.11.cloned.1.call-update) | async-done | bytes 2621456 | tf_op jit(solution)/shard_map/all_gather | solution.py:36
  301.6 7.4 %multiply_reduce_fusion.3 = (f32[1024]{0:T(1024)S(1)}, f32[1024,1024]{1,0:T(8,128)}) fusion(f32[]{:T(128)} %bitcast.10, bf16[1024,1280]{1,0:T(8,128)(2,1)} %all-gather.9.cloned.1.call-done, bf16[1024,1280]{1,0:T(8,128)(2,1)} %all-gather.11.cloned.1.call-done), kind=kOutput, calls=%fused_computation.11 | convolution fusion | flops 2686450688 | bytes 9441284 | tf_op jit(solution)/shard_map/dot_general | solution.py:54
  309.0 33.9 %all-reduce.4 = (f32[1024]{0:T(1024)S(1)}, f32[1024]{0:T(1024)S(1)}) all-reduce(f32[1024]{0:T(1024)S(1)} %get-tuple-element.25, f32[1024]{0:T(1024)S(1)} %get-tuple-element.27), channel_id=1, replica_groups=mesh['grp'=16,'dev'=16] {'grp'}, use_global_device_ids=true, to_apply=%region_9.0 | all-reduce | flops 2048 | bytes 16384 | tf_op jit(solution)/shard_map/pmax | solution.py:12
  342.9 4.5 exponential_reduce_fusion.1
  347.4 31.7 %all-reduce.2 = (f32[1024]{0:T(1024)S(1)}, f32[1024]{0:T(1024)S(1)}) all-reduce(f32[1024]{0:T(1024)S(1)} %get-tuple-element.8, f32[1024]{0:T(1024)S(1)} %get-tuple-element.30), channel_id=1, replica_groups=mesh['grp'=16,'dev'=16] {'grp'}, use_global_device_ids=true, to_apply=%region_11.0 | all-reduce | flops 2048 | bytes 16384 | tf_op jit(solution)/shard_map/psum | solution.py:13
  379.2 0.6 fusion.3
  379.8 56.5 %all-reduce.3 = (f32[1024]{0:T(1024)S(1)}, f32[1024]{0:T(1024)S(1)}) all-reduce(f32[1024]{0:T(1024)S(1)} %get-tuple-element.9, f32[1024]{0:T(1024)S(1)} %get-tuple-element.29), channel_id=1, replica_groups=mesh['grp'=16,'dev'=16] {'dev'}, use_global_device_ids=true, to_apply=%region_13.0 | all-reduce | flops 2048 | bytes 16384 | tf_op jit(solution)/shard_map/pmax | solution.py:20
  436.3 0.0 copy-start
  436.3 3.1 exponential_reduce_fusion
  439.4 0.4 copy-done
  439.7 0.7 exponential_reduce_fusion.2
  440.5 43.4 %all-reduce.1 = (f32[1024]{0:T(1024)S(1)}, f32[1024]{0:T(1024)S(1)}) all-reduce(f32[1024]{0:T(1024)S(1)} %exponential_reduce_fusion, f32[1024]{0:T(1024)S(1)} %exponential_reduce_fusion.2), channel_id=1, replica_groups=mesh['grp'=16,'dev'=16] {'dev'}, use_global_device_ids=true, to_apply=%region_15.0 | all-reduce | flops 2048 | bytes 16384 | tf_op jit(solution)/shard_map/psum | solution.py:21
  483.8 0.6 fusion.2
  484.4 0.0 copy-start.2
  484.4 8.1 %multiply_reduce_fusion = (f32[]{:T(128)}, f32[]{:T(128)}, f32[1024,1024]{1,0:T(8,128)S(1)}) fusion(f32[1024,1024]{1,0:T(8,128)} %get-tuple-element.28, f32[]{:T(128)} %bitcast.18, f32[1024]{0:T(1024)S(1)} %log_add_fusion, f32[1024]{0:T(1024)S(1)} %log_add_fusion.1, f32[1024,1024]{1,0:T(8,128)} %get-tuple-element.26, f32[]{:T(128)} %bitcast.13, ...), kind=kLoop, calls=%fused_computation | loop fusion | flops 14680062 | bytes 12599312 | tf_op jit(solution)/shard_map/reduce_sum | solution.py:101
  492.5 0.0 copy-start.1
  492.5 1.9 copy-done.1
  494.4 0.0 copy-done.2
  494.4 0.0 copy-start.3
  494.4 2.6 fusion
  497.0 0.0 reduce-scatter.5.cloned.1.call-update
  497.1 0.0 reduce-scatter.3.cloned.1.call-start
  497.1 0.0 copy-done.3
  497.1 4.8 fusion.1
  501.9 0.0 reduce-scatter.3.cloned.1.call-update
  503.8 79.2 %all-reduce = (f32[]{:T(128)}, f32[]{:T(128)}) all-reduce(f32[]{:T(128)S(6)} %sub.91, f32[]{:T(128)} %get-tuple-element.4), channel_id=1, replica_groups=mesh['grp'=16,'dev'=16] {'grp','dev'}, use_global_device_ids=true, to_apply=%region_21.0 | all-reduce | flops 2 | bytes 16 | tf_op jit(solution)/shard_map/psum | solution.py:102
  584.3 0.0 reduce-scatter.5.cloned.1.call-done
  584.3 70.8 %reduce-scatter.3.cloned.1.call-done = f32[64,512]{1,0:T(8,128)} async-done(((f32[1024,512]{1,0:T(8,128)}), f32[64,512]{1,0:T(8,128)}) %reduce-scatter.3.cloned.1.call-update) | async-done | bytes 131088 | tf_op jit(solution)/shard_map/reduce_scatter | solution.py:42
  (2 shorter events, 0.0 us)
Async XLA Ops:
  7.2 77.2 %all-gather.5.cloned.1.call-start = ((), (), s32[]{:S(2)}) async-start(), calls=%async_computation.2 | async-start | bytes 1114112 | tf_op jit(solution)/shard_map/all_gather | solution.py:30
  7.9 143.8 %all-gather.7.cloned.1.call-start = ((), (), s32[]{:S(2)}) async-start(), calls=%async_computation.3 | async-start | bytes 1114112 | tf_op jit(solution)/shard_map/all_gather | solution.py:37
  8.6 215.2 %all-gather.9.cloned.1.call-start = ((), (), s32[]{:S(2)}) async-start(), calls=%async_computation.4 | async-start | bytes 2785280 | tf_op jit(solution)/shard_map/all_gather | solution.py:29
  9.4 292.2 %all-gather.11.cloned.1.call-start = ((), (), s32[]{:S(2)}) async-start(), calls=%async_computation.5 | async-start | bytes 2785280 | tf_op jit(solution)/shard_map/all_gather | solution.py:36
  10.0 574.4 %reduce-scatter.5.cloned.1.call-start = ((), (), s32[]{:S(2)}) async-start(), calls=%async_computation.7 | async-start | bytes 2228224 | tf_op jit(solution)/shard_map/reduce_scatter | solution.py:48
  436.3 3.5 copy-start
  484.4 10.0 %copy-start.2 = (bf16[1024,512]{1,0:T(8,128)(2,1)S(1)}, bf16[1024,512]{1,0:T(8,128)(2,1)}, u32[]{:S(2)}) copy-start(bf16[1024,512]{1,0:T(8,128)(2,1)} %all-gather.5.cloned.1.call-done) | copy-start | bytes 3145732
  492.5 1.9 copy-start.1
  494.4 2.7 copy-start.3
  497.1 158.0 %reduce-scatter.3.cloned.1.call-start = ((), (), s32[]{:S(2)}) async-start(), calls=%async_computation.6 | async-start | bytes 2228224 | tf_op jit(solution)/shard_map/reduce_scatter | solution.py:42
Sparse Core Ops, SparseCore 0:
  9.8 74.5 all-gather.4
  87.0 64.6 all-gather.6
  153.5 70.2 all-gather.8
  226.4 75.1 all-gather.10
  497.2 79.6 reduce-scatter.4
  579.8 75.2 reduce-scatter.2
where the time goes:
time: 674 us; the launch traced here: 664 us
  waiting for transfers between devices  359 us (53%)
  blocking collectives  245 us (36%)
  between operations  20.9 us (3%)
  matrix products  19.5 us (3%)
  other arithmetic  17.6 us (3%)
    psum x1, blocking collectives, finish(): loss_total, scale_total = lax.psum((loss_part, scale_part), ('grp', 'dev'))  79.2 us
    all_gather x1, waiting for transfers between devices, gather_dev(): lax.all_gather(teacher_rows, 'dev', axis=0, tiled=True)  77.8 us
    all_gather x1, waiting for transfers between devices, gather_grp(): lax.all_gather(student_rows, 'grp', axis=0, tiled=True)  73.1 us
    reduce_scatter x1, waiting for transfers between devices, back_grp(): lax.psum_scatter(terms(jnp.int32(0), rows * lax.axis_size('grp')), 'grp',...  70.8 us
    all_gather x1, waiting for transfers between devices, gather_dev(): lax.all_gather(student_rows, 'dev', axis=0, tiled=True)  67.4 us
    all_gather x1, waiting for transfers between devices, gather_grp(): lax.all_gather(teacher_rows, 'grp', axis=0, tiled=True)  67.3 us
    pmax x1, blocking collectives, lse_dev(): lax.pmax((jnp.max(teacher, axis=dim), jnp.max(student, axis=dim)), 'dev')  56.5 us
    psum x1, blocking collectives, lse_dev(): lax.psum((exp_total(teacher, tpeak, dim), exp_total(student, speak, dim))...  43.4 us
  transfers between devices with their start and end apart: 6, of which 5 were waited for; matrix products, arithmetic and copies ran while one was open for 1% of the time, Pallas kernels for 0%

commit v1 on v0

v1 whole, which is shorter than its diff:
```python
import functools

import jax
import jax.numpy as jnp
from jax import lax
from jax.experimental import pallas as pl
from jax.experimental.pallas import tpu as pltpu
from jax.sharding import PartitionSpec as P

NX, NY, NZ = 4, 4, 8
ROWS = 64
TW, SW = 1280, 512
W = TW + SW
TILE = 1024
CHUNK = 256
SUB = 64
LOG2E = 1.4426950408889634
LN2 = 0.6931471805599453
MESH = pl.DeviceIdType.MESH
NT = (((1,), (1,)), ((), ()))
TN = (((0,), (0,)), ((), ()))


def kernel(
    ti, tt, si, st, tscale, sscale,
    gi_out, gt_out, loss_out, gs_out,
    img, txt, dtmp, ert, ect, ers, ecs, ds, wts,
    mrow, arow, lrow, cmax, csum, bcol,
    rst, cst, rst_in, cst_in,
    gi_own, gi_snd, gi_in, gt_all, gt_sib, gt_own, gt_snd, gt_in,
    sc_snd, sc_a, sc_mid, sc_b,
    loc_sem, ps_s, ps_r, zs_s, zs_r, cs_s, cs_r,
    rx_s, rx_r, cx_s, cx_r, gi_s, gi_r, sb_s, sb_r, gt_s, gt_r,
    sa_s, sa_r, sb2_s, sb2_r,
):
    g, d = lax.axis_index("grp"), lax.axis_index("dev")
    x, y, z, c = g % 4, d // 4, ((d // 2) % 2) * 4 + g // 4, d % 2
    me_p, me_c = y * 4 + x, z * 2 + c
    sib = 1 - c

    def at(xx, yy, zz, cc):
        return ((zz % 4) * 4 + xx, yy * 4 + (zz // 4) * 2 + cc)

    plane = [(dx, dy) for dy in range(NY) for dx in range(NX) if (dx, dy) != (0, 0)]
    column = [(dz, dc) for dz in range(NZ) for dc in range(2) if (dz, dc) != (0, 0)]

    def plane_peer(dx, dy):
        px, py = (x + dx) % NX, (y + dy) % NY
        return py * 4 + px, at(px, py, z, c)

    def column_peer(dz, dc):
        pz, pc = (z + dz) % NZ, (c + dc) % 2
        return pz * 2 + pc, at(x, y, pz, pc)

    local = []
    for k, (src, dst) in enumerate((
        (ti, img.at[y, x, :, pl.ds(0, TW)]),
        (si, img.at[y, x, :, pl.ds(TW, SW)]),
        (tt, txt.at[z, c, :, pl.ds(0, TW)]),
        (st, txt.at[z, c, :, pl.ds(TW, SW)]),
    )):
        cp = pltpu.make_async_copy(src, dst, loc_sem.at[k])
        cp.start()
        local.append(cp)

    barrier = pltpu.get_barrier_semaphore()
    for dx, dy in plane:
        pl.semaphore_signal(barrier, inc=1, device_id=plane_peer(dx, dy)[1], device_id_type=MESH)
    for dz, dc in column:
        pl.semaphore_signal(barrier, inc=1, device_id=column_peer(dz, dc)[1], device_id_type=MESH)
    for cp in local:
        cp.wait()
    pl.semaphore_wait(barrier, len(plane) + len(column))

    sent = []

    def send(src, dst, ssem, rsem, dev):
        cp = pltpu.make_async_remote_copy(
            src_ref=src, dst_ref=dst, send_sem=ssem, recv_sem=rsem, device_id=dev, device_id_type=MESH
        )
        cp.start()
        sent.append(cp)

    def arrived(dst, ssem, rsem, dev):
        pltpu.make_async_remote_copy(
            src_ref=dst, dst_ref=dst, send_sem=ssem, recv_sem=rsem, device_id=dev, device_id_type=MESH
        ).wait_recv()

    first, second = (x, y), (y, x)

    def region(h, a, b, r0, n):
        return img.at[b if h == 0 else a, a if h == 0 else b, pl.ds(32 * h + r0, n)]

    def chip(h, a, b):
        return at(a, b, z, c) if h == 0 else at(b, a, z, c)

    def sem_id(h, stage, sign, k):
        return 20 * h + (0, 2, 4, 12)[stage] + (sign > 0) + 2 * k

    def psend(h, stage, sign, k, reg, dev):
        i = sem_id(h, stage, sign, k)
        send(reg, reg, ps_s.at[i], ps_r.at[i], dev)

    def pwait(h, stage, sign, k, reg, dev):
        i = sem_id(h, stage, sign, k)
        arrived(reg, ps_s.at[i], ps_r.at[i], dev)

    def step(v, s, n):
        return (v + s + n) % n

    def a_of(h, k):
        return step(first[h], (0, -1, 1, 2)[k], 4)

    def t1_send(h, k):
        a, b = a_of(h, k), second[h]
        for sign in (1, -1):
            psend(h, 2, sign, k, region(h, a, b, 0, 32), chip(h, first[h], step(b, sign, 4)))

    def t1_recv(h, k):
        a, b = a_of(h, k), second[h]
        for sign in (1, -1):
            src = step(b, -sign, 4)
            pwait(h, 2, sign, k, region(h, a, src, 0, 32), chip(h, first[h], src))
            psend(h, 3, sign, k, region(h, a, src, 0 if sign > 0 else 16, 16), chip(h, first[h], step(b, sign, 4)))

    def t2_recv(h, k):
        a, b = a_of(h, k), second[h]
        for sign in (1, -1):
            pwait(h, 3, sign, k, region(h, a, step(b, 2, 4), 0 if sign > 0 else 16, 16), chip(h, first[h], step(b, -sign, 4)))

    def z_send(sign, s):
        zz = step(z, -sign * (s - 1), 8)
        reg = txt.at[zz, c] if s < 4 else txt.at[zz, c, pl.ds(0 if sign > 0 else 32, 32)]
        i = (s - 1) * 2 + (sign > 0)
        send(reg, reg, zs_s.at[i], zs_r.at[i], at(x, y, step(z, sign, 8), c))

    def z_recv(sign, s):
        zz = step(z, -sign * s, 8)
        reg = txt.at[zz, c] if s < 4 else txt.at[zz, c, pl.ds(0 if sign > 0 else 32, 32)]
        i = (s - 1) * 2 + (sign > 0)
        arrived(reg, zs_s.at[i], zs_r.at[i], at(x, y, step(z, -sign, 8), c))

    def c_send(dz):
        zz = step(z, dz, 8)
        send(txt.at[zz, c], txt.at[zz, c], cs_s.at[dz % 8], cs_r.at[dz % 8], at(x, y, z, sib))

    def c_recv(dz):
        zz = step(z, dz, 8)
        arrived(txt.at[zz, sib], cs_s.at[dz % 8], cs_r.at[dz % 8], at(x, y, z, sib))

    for h in (0, 1):
        for sign in (1, -1):
            psend(h, 0, sign, 0, region(h, first[h], second[h], 0, 32), chip(h, step(first[h], sign, 4), second[h]))
    for sign in (1, -1):
        z_send(sign, 1)
    c_send(0)
    for h in (0, 1):
        t1_send(h, 0)
    for h in (0, 1):
        for k, sign in ((1, 1), (2, -1)):
            src = step(first[h], -sign, 4)
            pwait(h, 0, sign, 0, region(h, src, second[h], 0, 32), chip(h, src, second[h]))
            psend(h, 1, sign, 0, region(h, src, second[h], 0 if sign > 0 else 16, 16), chip(h, step(first[h], sign, 4), second[h]))
            t1_send(h, k)
    for sign in (1, -1):
        z_recv(sign, 1)
        z_send(sign, 2)
        c_send(-sign)
    for h in (0, 1):
        t1_recv(h, 0)
    for h in (0, 1):
        for sign in (1, -1):
            pwait(h, 1, sign, 0, region(h, step(first[h], 2, 4), second[h], 0 if sign > 0 else 16, 16), chip(h, step(first[h], -sign, 4), second[h]))
        t1_send(h, 3)
    for h in (0, 1):
        t1_recv(h, 1)
    for sign in (1, -1):
        z_recv(sign, 2)
        z_send(sign, 3)
        c_send(-2 * sign)
    for h in (0, 1):
        t1_recv(h, 2)
    for h in (0, 1):
        t1_recv(h, 3)
    for sign in (1, -1):
        z_recv(sign, 3)
        z_send(sign, 4)
        c_send(-3 * sign)
    for h in (0, 1):
        for k in range(4):
            t2_recv(h, k)
    for sign in (1, -1):
        z_recv(sign, 4)
    c_send(4)
    for dz in range(8):
        c_recv(dz)

    lt, ls = tscale[0] * LOG2E, sscale[0] * LOG2E

    def fold(v, op):
        return op(v.reshape(v.shape[0] // 8, 8, v.shape[1]), axis=0)

    def pass1(q, carry):
        for part, (lo, hi, scale, er, ec) in enumerate(((0, TW, lt, ert, ect), (TW, W, ls, ers, ecs))):
            left = img[q, :, :, lo:hi].reshape(CHUNK, hi - lo)
            right = txt[:, :, :, lo:hi].reshape(TILE, hi - lo)
            base = 0 if part == 0 else q * CHUNK
            raw = dtmp if part == 0 else ds
            raw[pl.ds(base, CHUNK), :] = lax.dot_general(left, right, NT, preferred_element_type=jnp.float32)

            def by_row(s, peak):
                rows = pl.ds(q * CHUNK + s * SUB, SUB)
                v = raw[pl.ds(base + s * SUB, SUB), :]
                m = jnp.max(v, axis=1, keepdims=True)
                e = jnp.exp2((v - m) * scale)
                er[rows, :] = e
                mrow[part, rows, :] = m * scale
                lrow[part, rows, :] = m * scale + jnp.log2(jnp.sum(e, axis=1, keepdims=True))
                return jnp.maximum(peak, fold(v, jnp.max))

            peak = lax.fori_loop(0, CHUNK // SUB, by_row, jnp.full((8, TILE), -jnp.inf, jnp.float32))
            peak = jnp.max(peak, axis=0, keepdims=True)

            def by_col(s, total):
                rows = pl.ds(q * CHUNK + s * SUB, SUB)
                e = jnp.exp2((raw[pl.ds(base + s * SUB, SUB), :] - peak) * scale)
                ec[rows, :] = e
                return total + fold(e, jnp.sum)

            total = lax.fori_loop(0, CHUNK // SUB, by_col, jnp.zeros((8, TILE), jnp.float32))
            cmax[part, q] = peak * scale
            csum[part, q] = jnp.sum(total, axis=0, keepdims=True)
        return carry

    lax.fori_loop(0, TILE // CHUNK, pass1, 0)

    eye = lax.broadcasted_iota(jnp.int32, (128, 128), 0) == lax.broadcasted_iota(jnp.int32, (128, 128), 1)
    for part in range(2):
        m = jnp.max(cmax[part], axis=0)
        total = jnp.sum(csum[part] * jnp.exp2(cmax[part] - m[None]), axis=0)
        lse = m + jnp.log2(total)
        for k in range(8):
            cst[pl.ds(part * 8 + k, 1), :] = lse[:, 128 * k:128 * k + 128]
    for dz, dc in column:
        i, dev = column_peer(dz, dc)
        send(cst, cst_in.at[me_c], cx_s.at[i], cx_r.at[me_c], dev)
    for part in range(2):
        for k in range(8):
            v = lrow[part, pl.ds(128 * k, 128), :]
            rst[pl.ds(part * 8 + k, 1), :] = jnp.sum(jnp.where(eye, v, 0.0), axis=0, keepdims=True)
    for dx, dy in plane:
        i, dev = plane_peer(dx, dy)
        send(rst, rst_in.at[me_p], rx_s.at[i], rx_r.at[me_p], dev)
    cst_in[me_c] = cst[...]
    rst_in[me_p] = rst[...]

    def total_lse(v):
        m = jnp.max(v, axis=0)
        return m + jnp.log2(jnp.sum(jnp.exp2(v - m[None]), axis=0))

    half = 0.5 * sscale[0]
    for dz, dc in column:
        i, dev = column_peer(dz, dc)
        arrived(cst_in.at[i], cx_s.at[i], cx_r.at[i], dev)
    col = total_lse(cst_in[...])
    for part in range(2):
        lse = jnp.concatenate([col[part * 8 + k:part * 8 + k + 1, :] for k in range(8)], axis=1)
        bcol[part] = half * jnp.exp2(cmax[part] - lse[None])
    for dx, dy in plane:
        i, dev = plane_peer(dx, dy)
        arrived(rst_in.at[i], rx_s.at[i], rx_r.at[i], dev)
    row = total_lse(rst_in[...])
    for part in range(2):
        for k in range(8):
            v = jnp.broadcast_to(row[part * 8 + k:part * 8 + k + 1, :], (128, 128))
            lse = jnp.sum(jnp.where(eye, v, 0.0), axis=1, keepdims=True)
            rows = pl.ds(128 * k, 128)
            arow[part, rows, :] = half * jnp.exp2(mrow[part, rows, :] - lse)

    def pass2(s, carry):
        loss_acc, scale_acc = carry
        rows = pl.ds(s * SUB, SUB)
        q = s // (CHUNK // SUB)
        v = ds[rows, :]
        teach = ert[rows, :] * arow[0, rows, :] + ect[rows, :] * bcol[0, q]
        stud = ers[rows, :] * arow[1, rows, :] + ecs[rows, :] * bcol[1, q]
        differ = stud - teach
        wts[rows, :] = differ.astype(jnp.bfloat16)
        return loss_acc + fold(teach * v, jnp.sum), scale_acc + fold(differ * v, jnp.sum)

    zero = jnp.zeros((8, TILE), jnp.float32)
    loss_acc, scale_acc = lax.fori_loop(0, TILE // SUB, pass2, (zero, zero))

    def narrow(v):
        return functools.reduce(jnp.add, [v[:, 128 * k:128 * k + 128] for k in range(8)])

    sc_snd[pl.ds(0, 8), :] = (row[8:, :] + col[8:, :]) * (LN2 / 16.0) - 2.0 * narrow(loss_acc)
    sc_snd[pl.ds(8, 8), :] = 2.0 * narrow(scale_acc)
    for dx, dy in plane:
        i, dev = plane_peer(dx, dy)
        send(sc_snd, sc_a.at[me_p], sa_s.at[i], sa_r.at[me_p], dev)

    for q in range(4):
        v = lax.dot_general(
            wts[:, 256 * q:256 * q + 256], img[:, :, :, TW:].reshape(TILE, SW), TN, preferred_element_type=jnp.float32
        )
        gt_all[pl.ds(2 * q, 2)] = v.reshape(2, 2, ROWS, SW)
    send(gt_all.at[:, sib], gt_sib, sb_s, sb_r, at(x, y, z, sib))

    for q in range(4):
        v = jnp.dot(
            wts[pl.ds(256 * q, 256), :], txt[:, :, :, TW:].reshape(TILE, SW), preferred_element_type=jnp.float32
        )
        gi_own[pl.ds(4 * q, 4)] = v.reshape(4, ROWS, SW)
        gi_snd[pl.ds(4 * q, 4)] = v.reshape(4, ROWS, SW).astype(jnp.bfloat16)
    for dx, dy in plane:
        i, dev = plane_peer(dx, dy)
        send(gi_snd.at[i], gi_in.at[me_p], gi_s.at[i], gi_r.at[me_p], dev)

    arrived(gt_sib, sb_s, sb_r, at(x, y, z, sib))
    for q in range(8):
        v = gt_all[q, c] + gt_sib[q]
        gt_own[q] = v
        gt_snd[q] = v.astype(jnp.bfloat16)
    for dz in range(1, 8):
        pz = (z + dz) % 8
        send(gt_snd.at[pz], gt_in.at[z], gt_s.at[pz], gt_r.at[z], at(x, y, pz, c))

    v = sc_snd[...]
    for dx, dy in plane:
        i, dev = plane_peer(dx, dy)
        arrived(sc_a.at[i], sa_s.at[i], sa_r.at[i], dev)
    sc_a[me_p] = v
    sc_mid[...] = jnp.sum(sc_a[...], axis=0)
    for dz, dc in column:
        i, dev = column_peer(dz, dc)
        send(sc_mid, sc_b.at[me_c], sb2_s.at[i], sb2_r.at[me_c], dev)

    gi_out[...] = gi_own[me_p]
    for dx, dy in plane:
        i, dev = plane_peer(dx, dy)
        arrived(gi_in.at[i], gi_s.at[i], gi_r.at[i], dev)
        gi_out[...] += gi_in[i].astype(jnp.float32)
    gt_out[...] = gt_own[z]
    for dz in range(1, 8):
        pz = (z + dz) % 8
        arrived(gt_in.at[pz], gt_s.at[pz], gt_r.at[pz], at(x, y, pz, c))
        gt_out[...] += gt_in[pz].astype(jnp.float32)
    for dz, dc in column:
        i, dev = column_peer(dz, dc)
        arrived(sc_b.at[i], sb2_s.at[i], sb2_r.at[i], dev)
    sc_b[me_c] = sc_mid[...]
    total = jnp.sum(sc_b[...], axis=0)
    pairs = 2.0 * TILE * 16
    loss_out[0] = jnp.sum(total[:8]) / pairs
    gs_out[0] = jnp.sum(total[8:]) / (pairs * sscale[0])
    for cp in sent:
        cp.wait_send()


def shards(*args):
    f32, bf16 = jnp.float32, jnp.bfloat16
    anyw = pl.BlockSpec(memory_space=pl.ANY)
    vmem = pl.BlockSpec(memory_space=pltpu.VMEM)
    smem = pl.BlockSpec(memory_space=pltpu.SMEM)
    sem = pltpu.SemaphoreType.DMA
    V = pltpu.VMEM
    return tuple(pl.pallas_call(
        kernel,
        out_shape=(
            jax.ShapeDtypeStruct((ROWS, SW), f32),
            jax.ShapeDtypeStruct((ROWS, SW), f32),
            jax.ShapeDtypeStruct((1,), f32),
            jax.ShapeDtypeStruct((1,), f32),
        ),
        in_specs=[anyw] * 4 + [smem] * 2,
        out_specs=(vmem, vmem, smem, smem),
        scratch_shapes=[
            V((NY, NX, ROWS, W), bf16),
            V((NZ, 2, ROWS, W), bf16),
            V((CHUNK, TILE), f32),
            V((TILE, TILE), f32),
            V((TILE, TILE), f32),
            V((TILE, TILE), f32),
            V((TILE, TILE), f32),
            V((TILE, TILE), f32),
            V((TILE, TILE), bf16),
            V((2, TILE, 1), f32),
            V((2, TILE, 1), f32),
            V((2, TILE, 1), f32),
            V((2, 4, 1, TILE), f32),
            V((2, 4, 1, TILE), f32),
            V((2, 4, 1, TILE), f32),
            V((16, 128), f32),
            V((16, 128), f32),
            V((16, 16, 128), f32),
            V((16, 16, 128), f32),
            V((16, ROWS, SW), f32),
            V((16, ROWS, SW), bf16),
            V((16, ROWS, SW), bf16),
            V((8, 2, ROWS, SW), f32),
            V((8, ROWS, SW), f32),
            V((8, ROWS, SW), f32),
            V((8, ROWS, SW), bf16),
            V((8, ROWS, SW), bf16),
            V((16, 128), f32),
            V((16, 16, 128), f32),
            V((16, 128), f32),
            V((16, 16, 128), f32),
            sem((4,)),
            sem((40,)), sem((40,)),
            sem((8,)), sem((8,)),
            sem((8,)), sem((8,)),
            sem((16,)), sem((16,)),
            sem((16,)), sem((16,)),
            sem((16,)), sem((16,)),
            sem, sem,
            sem((8,)), sem((8,)),
            sem((16,)), sem((16,)),
            sem((16,)), sem((16,)),
        ],
        compiler_params=pltpu.CompilerParams(
            collective_id=0, has_side_effects=True, vmem_limit_bytes=60 * 1024 * 1024
        ),
    )(*args))


def solution(mesh):
    return jax.shard_map(
        shards,
        mesh=mesh,
        in_specs=(
            P(("grp", "dev"), None),
            P(("grp", "dev"), None),
            P(("grp", "dev"), None),
            P(("grp", "dev"), None),
            P(),
            P(),
        ),
        out_specs=(P(("grp", "dev"), None), P(("grp", "dev"), None), P(), P()),
        check_vma=False,
    )
```

time: 674 us -> 92.1 us (0.14); the launches traced: 664 us -> 91.9 us
  waiting for transfers between devices: 359 us -> 0 us
  blocking collectives: 245 us -> 0 us
  Pallas kernels: 0 us -> 84.2 us
  matrix products: 19.5 us -> 0 us
  other arithmetic: 17.6 us -> 0 us
  between operations: 20.9 us -> 5.43 us
    all_gather x4 -> x0, waiting for transfers between devices: 286 us -> none  [the longest x1 77.8 us: gather_dev(): lax.all_gather(teacher_rows, 'dev', axis=0, tiled=True)]
    psum x3 -> x0, blocking collectives: 154 us -> none  [the longest x1 79.2 us: finish(): loss_total, scale_total = lax.psum((loss_part, scale_part), ('grp', 'dev'))]
    pmax x2 -> x0, blocking collectives: 90.4 us -> none  [the longest x1 56.5 us: lse_dev(): lax.pmax((jnp.max(teacher, axis=dim), jnp.max(student, axis=dim)), 'dev')]
    pallas_call x0 -> x1, Pallas kernels: none -> 84.2 us  [shards(): pl.pallas_call(kernel, out_shape=(jax.ShapeDtypeStruct((ROWS, SW), f32),...]
    reduce_scatter x2 -> x0, waiting for transfers between devices: 70.8 us -> none  [the longest x1 70.8 us: back_grp(): lax.psum_scatter(terms(jnp.int32(0), rows * lax.axis_size('grp')), 'grp',...]
    dot_general x4 -> x0, matrix products: 19.5 us -> none  [the longest x2 12.1 us: pair_dot(): lax.dot_general(left, right, (((1,), (1,)), ((), ())), preferred_element_...]
    reduce_sum x6 -> x0, other arithmetic: 17.6 us -> none  [the longest x3 8.32 us: exp_total(): return jnp.sum(jnp.exp(values - jnp.expand_dims(peak, dim)), axis=dim)]
  transfers between devices with their start and end apart: 6 -> 0, of which waited for: 5 -> 0; matrix products, arithmetic and copies ran while one was open for 1% -> 0% of each run, Pallas kernels for 0% -> 0%
where the time goes in v1:
time: 92.1 us; the launch traced here: 91.9 us
  Pallas kernels  84.2 us (91%)
  between operations  5.43 us (6%)
  local copies, waits for them, and re-layouts  2.26 us (2%)
    pallas_call x1, Pallas kernels, shards(): pl.pallas_call(kernel, out_shape=(jax.ShapeDtypeStruct((ROWS, SW), f32),...  84.2 us
    unnamed x4, local copies, waits for them, and re-layouts  2.26 us

profile of v1, /device:TPU:1, one launch (start us, length us, event | category | flops | bytes accessed | tf_op | source)
XLA Modules:
  0.0 91.9 jit_solution(508190569214889114)
XLA Ops:
  1.9 84.2 %shard_map.93 = (f32[64,512]{1,0:T(8,128)}, f32[64,512]{1,0:T(8,128)}, f32[1]{0:T(128)}, f32[1]{0:T(128)}) custom-call(bf16[64,1280]{1,0:T(8,128)(2,1)} %ti.1, bf16[64,1280]{1,0:T(8,128)(2,1)} %tt.1, bf16[64,512]{1,0:T(8,128)(2,1)} %si.1, bf16[64,512]{1,0:T(8,128)(2,1)} %st.1, f32[1]{0:T(128)S(6)} %copy.14.tscale, f32[1]{0:T(128)S(6)} %copy.15.sscale), custom_call_target="tpu_custom_call" | custom-call | tf_op jit(solution)/shard_map/pallas_call | solution.py:368
  86.1 0.0 copy-start
  86.2 1.6 %copy.16 = f32[64,512]{1,0:T(8,128)} copy(f32[64,512]{1,0:T(8,128)} %get-tuple-element.8) | data formatting | bytes 262144
  87.8 0.0 copy-done
  87.8 0.7 copy.17
Async XLA Ops:
  86.1 1.6 %copy-start = (f32[64,512]{1,0:T(8,128)S(1)}, f32[64,512]{1,0:T(8,128)}, u32[]{:S(2)}) copy-start(f32[64,512]{1,0:T(8,128)} %get-tuple-element.9) | copy-start | bytes 393220

commit v2 on v1

v2 whole, which is shorter than its diff:
```python
import functools

import jax
import jax.numpy as jnp
from jax import lax
from jax.experimental import pallas as pl
from jax.experimental.pallas import tpu as pltpu
from jax.sharding import PartitionSpec as P

NX, NY, NZ = 4, 4, 8
ROWS = 64
TW, SW = 1280, 512
W = TW + SW
TILE = 1024
CHUNK = 256
LOG2E = 1.4426950408889634
LN2 = 0.6931471805599453
MESH = pl.DeviceIdType.MESH
NT = (((1,), (1,)), ((), ()))
TN = (((0,), (0,)), ((), ()))

A_OF = (0, 3, 1, 2)
SLOT = (0, 1, 3, 5, 7, 6, 4, 2)
STRIPS = ((0, 512), (512, 256), (768, 256))
LAST = ((0, 512), (512, 512))


def row_unit(h, a, b):
    k = A_OF.index(a)
    if b == 0:
        return 128 * h + 32 * a
    if b == 2:
        return 768 + 64 * k + 32 * h
    return 256 + 128 * k + (0 if b == 3 else 64) + 32 * h


UNITS = tuple((h, a, b, row_unit(h, a, b)) for h in range(2) for a in range(4) for b in range(4))


def lanes(v, op):
    return functools.reduce(op, [v[:, 128 * k:128 * k + 128] for k in range(v.shape[1] // 128)])


def sublanes(v, op):
    return functools.reduce(op, [v[8 * k:8 * k + 8] for k in range(v.shape[0] // 8)])


def wide(v, n):
    return jnp.concatenate([v] * n, axis=1)


def tall(v, n):
    return jnp.concatenate([v] * n, axis=0)


def kernel(
    ti, tt, si, st, tscale, sscale,
    gi_out, gt_out, loss_out, gs_out,
    img, txt, vt, vs, ert, ect, ers, ecs, wts,
    rmax, rsum, cmax, csum, rel, rst, cst, rall, call, rst_in, cst_in,
    gi_own, gi_snd, gi_in, gt_all, gt_sib, gt_own, gt_snd, gt_in,
    sc_snd, sc_a, sc_mid, sc_b,
    loc_sem, ps_s, ps_r, zs_s, zs_r, cs_s, cs_r,
    rx_s, rx_r, cx_s, cx_r, gi_s, gi_r, sb_s, sb_r, gt_s, gt_r,
    sa_s, sa_r, sb2_s, sb2_r,
):
    g, d = lax.axis_index("grp"), lax.axis_index("dev")
    x, y, z, c = g % 4, d // 4, ((d // 2) % 2) * 4 + g // 4, d % 2
    me_p, me_c = y * 4 + x, z * 2 + c
    sib = 1 - c

    def at(xx, yy, zz, cc):
        return ((zz % 4) * 4 + xx, yy * 4 + (zz // 4) * 2 + cc)

    plane = [(dx, dy) for dy in range(NY) for dx in range(NX) if (dx, dy) != (0, 0)]
    column = [(dz, dc) for dz in range(NZ) for dc in range(2) if (dz, dc) != (0, 0)]

    def plane_peer(dx, dy):
        px, py = (x + dx) % NX, (y + dy) % NY
        return py * 4 + px, at(px, py, z, c)

    def column_peer(dz, dc):
        pz, pc = (z + dz) % NZ, (c + dc) % 2
        return pz * 2 + pc, at(x, y, pz, pc)

    def along(h, axis, step):
        if (h + axis) % 2 == 0:
            return at((x + step) % NX, y, z, c)
        return at(x, (y + step) % NY, z, c)

    def up(step):
        return at(x, y, (z + step) % NZ, c)

    other = at(x, y, z, sib)

    local = []

    def bring(src, dst):
        cp = pltpu.make_async_copy(src, dst, loc_sem.at[len(local)])
        cp.start()
        local.append(cp)

    for h in range(2):
        r = row_unit(h, 0, 0)
        bring(ti.at[pl.ds(32 * h, 32)], img.at[pl.ds(r, 32), pl.ds(0, TW)])
        bring(si.at[pl.ds(32 * h, 32)], img.at[pl.ds(r, 32), pl.ds(TW, SW)])
    bring(tt, txt.at[0, c, :, pl.ds(0, TW)])
    bring(st, txt.at[0, c, :, pl.ds(TW, SW)])

    barrier = pltpu.get_barrier_semaphore()
    near = [along(0, axis, step) for axis in range(2) for step in (1, -1)] + [up(1), up(-1), other]
    for dev in near:
        pl.semaphore_signal(barrier, inc=1, device_id=dev, device_id_type=MESH)
    for cp in local:
        cp.wait()
    pl.semaphore_wait(barrier, len(near))

    sent = []

    def send(src, dst, ssem, rsem, dev):
        cp = pltpu.make_async_remote_copy(
            src_ref=src, dst_ref=dst, send_sem=ssem, recv_sem=rsem, device_id=dev, device_id_type=MESH
        )
        cp.start()
        sent.append(cp)

    def arrived(dst, ssem, rsem, dev):
        pltpu.make_async_remote_copy(
            src_ref=dst, dst_ref=dst, send_sem=ssem, recv_sem=rsem, device_id=dev, device_id_type=MESH
        ).wait_recv()

    both = (1, -1)

    def unit(h, a, b, r0=0, n=32):
        return img.at[pl.ds(row_unit(h, a % 4, b % 4) + r0, n)]

    def sem_id(h, stage, sign, k):
        return 20 * h + (0, 2, 4, 12)[stage] + (sign > 0) + 2 * k

    def psend(h, stage, sign, k, src, dst, axis):
        i = sem_id(h, stage, sign, k)
        send(src, dst, ps_s.at[i], ps_r.at[i], along(h, axis, sign))

    def pwait(h, stage, sign, k, dst, axis):
        i = sem_id(h, stage, sign, k)
        arrived(dst, ps_s.at[i], ps_r.at[i], along(h, axis, -sign))

    def half_of(sign):
        return (0 if sign > 0 else 16), 16

    def s1_send(h):
        for sign in both:
            psend(h, 0, sign, 0, unit(h, 0, 0), unit(h, -sign, 0), 0)

    def s1_recv(h):
        for sign in both:
            pwait(h, 0, sign, 0, unit(h, -sign, 0), 0)
            psend(h, 1, sign, 0, unit(h, -sign, 0, *half_of(sign)), unit(h, 2, 0, *half_of(sign)), 0)
        for sign in both:
            t1_send(h, 1 if sign > 0 else 2)

    def s2_recv(h):
        for sign in both:
            pwait(h, 1, sign, 0, unit(h, 2, 0, *half_of(sign)), 0)
        t1_send(h, 3)

    def t1_send(h, k):
        for sign in both:
            psend(h, 2, sign, k, unit(h, A_OF[k], 0), unit(h, A_OF[k], -sign), 1)

    def t1_recv(h, k):
        for sign in both:
            pwait(h, 2, sign, k, unit(h, A_OF[k], -sign), 1)
            psend(h, 3, sign, k, unit(h, A_OF[k], -sign, *half_of(sign)), unit(h, A_OF[k], 2, *half_of(sign)), 1)

    def t2_recv(h, k):
        for sign in both:
            pwait(h, 3, sign, k, unit(h, A_OF[k], 2, *half_of(sign)), 1)

    def zpart(dz, q):
        return txt.at[SLOT[dz % 8], c, pl.ds(32 * q, 32)]

    def first_half(sign):
        return 0 if sign > 0 else 1

    def z_move(sign, s, q):
        i = ((s - 1) * 2 + q) * 2 + (sign > 0)
        send(zpart(-sign * (s - 1), q), zpart(-sign * s, q), zs_s.at[i], zs_r.at[i], up(sign))

    def z_come(sign, s, q):
        i = ((s - 1) * 2 + q) * 2 + (sign > 0)
        arrived(zpart(-sign * s, q), zs_s.at[i], zs_r.at[i], up(-sign))

    def z_step(s, second):
        for sign in both:
            q = first_half(sign) ^ second
            z_come(sign, s, q)
            if s < 3 or not second:
                z_move(sign, s + 1, q)

    def c_move(dz):
        send(txt.at[SLOT[dz % 8], c], txt.at[SLOT[dz % 8], c], cs_s.at[dz % 8], cs_r.at[dz % 8], other)

    def c_come(dz):
        arrived(txt.at[SLOT[dz % 8], sib], cs_s.at[dz % 8], cs_r.at[dz % 8], other)

    lt, ls = tscale[0] * LOG2E, sscale[0] * LOG2E
    parts = ((0, TW, lt, vt, ert, ect), (TW, W, ls, vs, ers, ecs))

    def tile(q, strip, c0, n):
        r0 = q * CHUNK
        cols = pl.ds(c0, n)
        blocks = pl.ds(c0 // 128, n // 128)
        for part, (lo, hi, scale, raw, er, ec) in enumerate(parts):
            raw[pl.ds(r0, CHUNK), cols] = scale * lax.dot_general(
                img[pl.ds(r0, CHUNK), lo:hi],
                txt[blocks, :, :, lo:hi].reshape(n, hi - lo),
                NT,
                preferred_element_type=jnp.float32,
            )
            peak = None
            for s in range(CHUNK // 32):
                rows = pl.ds(r0 + 32 * s, 32)
                v = raw[rows, cols]
                m = lanes(v, jnp.maximum)
                e = jnp.exp2(v - wide(m, n // 128))
                er[rows, cols] = e
                rmax[part, strip, rows, :] = m
                rsum[part, strip, rows, :] = lanes(e, jnp.add)
                high = sublanes(v, jnp.maximum)
                peak = high if peak is None else jnp.maximum(peak, high)
            total = None
            for s in range(CHUNK // 32):
                rows = pl.ds(r0 + 32 * s, 32)
                e = jnp.exp2(raw[rows, cols] - tall(peak, 4))
                ec[rows, cols] = e
                add = sublanes(e, jnp.add)
                total = add if total is None else total + add
            cmax[part, q, :, cols] = peak
            csum[part, q, :, cols] = total

    def tiles(first, last, strip):
        def body(q, carry):
            tile(q, strip, *STRIPS[strip])
            return carry

        lax.fori_loop(first, last, body, 0)

    for h in range(2):
        s1_send(h)
    for second in range(2):
        for sign in both:
            z_move(sign, 1, first_half(sign) ^ second)
    c_move(0)
    for h in range(2):
        t1_send(h, 0)
    for h in range(2):
        s1_recv(h)
    z_step(1, 0)
    for h in range(2):
        t1_recv(h, 0)
    z_step(1, 1)
    for sign in both:
        c_move(sign)
    for h in range(2):
        s2_recv(h)
    z_step(2, 0)
    for h in range(2):
        t1_recv(h, 1)
    z_step(2, 1)
    for sign in both:
        c_move(2 * sign)
    for h in range(2):
        t1_recv(h, 2)
    for dz in (0, 1, -1, 2):
        c_come(dz)
    tiles(0, 1, 0)
    z_step(3, 0)
    for h in range(2):
        t2_recv(h, 0)
    tiles(1, 2, 0)
    for h in range(2):
        t1_recv(h, 3)
    z_step(3, 1)
    for sign in both:
        c_move(3 * sign)
    tiles(2, 3, 0)
    for dz in (-2, 3):
        c_come(dz)
    tiles(0, 3, 1)
    for sign in both:
        z_come(sign, 4, first_half(sign))
    c_move(4)
    for h in range(2):
        for k in (1, 2, 3):
            t2_recv(h, k)
    for dz in (-3, 4):
        c_come(dz)
    tiles(0, 3, 2)
    for strip, (c0, n) in enumerate(LAST):
        tile(3, strip, c0, n)

    for part in range(2):
        high = jnp.max(cmax[part], axis=0)
        high = jnp.max(high, axis=0, keepdims=True)
        total = jnp.sum(csum[part] * jnp.exp2(cmax[part] - high[None]), axis=0)
        lse = high + jnp.log2(jnp.sum(total, axis=0, keepdims=True))
        for dz in range(8):
            k = SLOT[dz]
            cst[pl.ds(part * 8 + (z + dz) % 8, 1), :] = lse[:, 128 * k:128 * k + 128]
    for dz, dc in column:
        i, dev = column_peer(dz, dc)
        send(cst, cst_in.at[me_c], cx_s.at[i], cx_r.at[me_c], dev)

    for part in range(2):
        for k in range(8):
            rows = pl.ds(128 * k, 128)
            strips = range(3 if k < 6 else 2)
            m = [rmax[part, s, rows, :] for s in strips]
            high = functools.reduce(jnp.maximum, m)
            total = functools.reduce(jnp.add, [rsum[part, s, rows, :] * jnp.exp2(m[s] - high) for s in strips])
            high, total = high.T, total.T
            peak = jnp.max(high, axis=0, keepdims=True)
            lse = peak + jnp.log2(jnp.sum(total * jnp.exp2(high - peak), axis=0, keepdims=True))
            for h, a, b, r in UNITS:
                if r // 128 == k:
                    o = r % 128
                    rel[pl.ds(part * 8 + h * 4 + b, 1), pl.ds(32 * a, 32)] = lse[:, o:o + 32]
        v = rel[pl.ds(part * 8, 8), :]
        v = (pltpu.roll(v, 32 * x, axis=1), pltpu.roll(v, 32 * y, axis=1))
        for h in range(2):
            for b in range(4):
                k = h * 4 + b
                rst[pl.ds(part * 8 + h * 4 + (b + (y, x)[h]) % 4, 1), :] = v[h][k:k + 1]
    for dx, dy in plane:
        i, dev = plane_peer(dx, dy)
        send(rst, rst_in.at[me_p], rx_s.at[i], rx_r.at[me_p], dev)
    cst_in[me_c] = cst[...]
    rst_in[me_p] = rst[...]

    def total_lse(v):
        m = jnp.max(v, axis=0)
        return m + jnp.log2(jnp.sum(jnp.exp2(v - m[None]), axis=0))

    half = 0.5 * sscale[0]
    for dz, dc in column:
        i, dev = column_peer(dz, dc)
        arrived(cst_in.at[i], cx_s.at[i], cx_r.at[i], dev)
    col = total_lse(cst_in[...])
    call[...] = col
    for part in range(2):
        lse = [None] * 8
        for dz in range(8):
            lse[SLOT[dz]] = call[pl.ds(part * 8 + (z + dz) % 8, 1), :]
        cmax[part] = half * jnp.exp2(cmax[part] - jnp.concatenate(lse, axis=1)[None])
    for dx, dy in plane:
        i, dev = plane_peer(dx, dy)
        arrived(rst_in.at[i], rx_s.at[i], rx_r.at[i], dev)
    row = total_lse(rst_in[...])
    rall[...] = row
    for part in range(2):
        for h in range(2):
            for b in range(4):
                rel[pl.ds(part * 8 + h * 4 + b, 1), :] = rall[pl.ds(part * 8 + h * 4 + (b + (y, x)[h]) % 4, 1), :]
        v = rel[pl.ds(part * 8, 8), :]
        v = (pltpu.roll(v, 128 - 32 * x, axis=1), pltpu.roll(v, 128 - 32 * y, axis=1))
        for k in range(8):
            mine = sorted((r, h, a, b) for h, a, b, r in UNITS if r // 128 == k)
            lse = jnp.concatenate(
                [v[h][h * 4 + b:h * 4 + b + 1, 32 * a:32 * a + 32] for _, h, a, b in mine], axis=1
            )
            lse = jnp.broadcast_to(lse, (128, 128)).T
            rows = pl.ds(128 * k, 128)
            for s in range(3 if k < 6 else 2):
                rmax[part, s, rows, :] = half * jnp.exp2(rmax[part, s, rows, :] - lse)

    def pass2(strips):
        def body(s, carry):
            loss_acc, scale_acc = carry
            rows = pl.ds(pl.multiple_of(s * 32, 32), 32)
            q = s // (CHUNK // 32)
            for strip, (c0, n) in enumerate(strips):
                cols = pl.ds(c0, n)
                v = vs[rows, cols]
                k = n // 128
                teach = ert[rows, cols] * wide(rmax[0, strip, rows, :], k) + ect[rows, cols] * tall(cmax[0, q, :, cols], 4)
                stud = ers[rows, cols] * wide(rmax[1, strip, rows, :], k) + ecs[rows, cols] * tall(cmax[1, q, :, cols], 4)
                differ = stud - teach
                wts[rows, cols] = differ.astype(jnp.bfloat16)
                loss_acc = loss_acc + lanes(sublanes(teach * v, jnp.add), jnp.add)
                scale_acc = scale_acc + lanes(sublanes(differ * v, jnp.add), jnp.add)
            return loss_acc, scale_acc

        return body

    zero = jnp.zeros((8, 128), jnp.float32)
    accs = lax.fori_loop(0, 24, pass2(STRIPS), (zero, zero), unroll=2)
    loss_acc, scale_acc = lax.fori_loop(24, 32, pass2(LAST), accs, unroll=2)

    back = LN2 / half
    sc_snd[pl.ds(0, 8), :] = (row[8:, :] + col[8:, :]) * (LN2 / 16.0) - loss_acc * back
    sc_snd[pl.ds(8, 8), :] = scale_acc * back
    for dx, dy in plane:
        i, dev = plane_peer(dx, dy)
        send(sc_snd, sc_a.at[me_p], sa_s.at[i], sa_r.at[me_p], dev)

    for q in (3, 2, 1, 0):
        v = lax.dot_general(
            wts[:, 256 * q:256 * q + 256], img[:, TW:], TN, preferred_element_type=jnp.float32
        )
        pair = pl.ds(2 * q, 2)
        gt_all[pair] = v.reshape(2, 2, ROWS, SW)
        send(gt_all.at[pair, sib], gt_sib.at[pair], sb_s.at[q], sb_r.at[q], other)

    for q in range(4):
        v = jnp.dot(
            wts[pl.ds(256 * q, 256), :], txt[:, :, :, TW:].reshape(TILE, SW), preferred_element_type=jnp.float32
        )
        for h, a, b, r in UNITS:
            if r // 256 == q:
                o = r % 256
                place = (b * 4 + a) if h == 0 else (a * 4 + b)
                gi_snd[place, pl.ds(32 * h, 32), :] = v[o:o + 32].astype(jnp.bfloat16)
                if place == 0:
                    gi_own[pl.ds(32 * h, 32), :] = v[o:o + 32]
    for dx, dy in plane:
        i, dev = plane_peer(dx, dy)
        send(gi_snd.at[dy * 4 + dx], gi_in.at[me_p], gi_s.at[i], gi_r.at[me_p], dev)

    for q in (3, 2, 1, 0):
        pair = pl.ds(2 * q, 2)
        arrived(gt_sib.at[pair], sb_s.at[q], sb_r.at[q], other)
        for dz in range(8):
            k = SLOT[dz]
            if k // 2 == q:
                v = gt_all[k, c] + gt_sib[k]
                if dz == 0:
                    gt_own[...] = v
                else:
                    gt_snd[k] = v.astype(jnp.bfloat16)
                    pz = (z + dz) % 8
                    send(gt_snd.at[k], gt_in.at[z], gt_s.at[pz], gt_r.at[z], at(x, y, pz, c))

    v = sc_snd[...]
    for dx, dy in plane:
        i, dev = plane_peer(dx, dy)
        arrived(sc_a.at[i], sa_s.at[i], sa_r.at[i], dev)
    sc_a[me_p] = v
    sc_mid[...] = jnp.sum(sc_a[...], axis=0)
    for dz, dc in column:
        i, dev = column_peer(dz, dc)
        send(sc_mid, sc_b.at[me_c], sb2_s.at[i], sb2_r.at[me_c], dev)

    gi_out[...] = gi_own[...]
    for dx, dy in plane:
        i, dev = plane_peer(dx, dy)
        arrived(gi_in.at[i], gi_s.at[i], gi_r.at[i], dev)
        gi_out[...] += gi_in[i].astype(jnp.float32)
    gt_out[...] = gt_own[...]
    for dz in range(1, 8):
        pz = (z + dz) % 8
        arrived(gt_in.at[pz], gt_s.at[pz], gt_r.at[pz], at(x, y, pz, c))
        gt_out[...] += gt_in[pz].astype(jnp.float32)
    for dz, dc in column:
        i, dev = column_peer(dz, dc)
        arrived(sc_b.at[i], sb2_s.at[i], sb2_r.at[i], dev)
    sc_b[me_c] = sc_mid[...]
    total = jnp.sum(sc_b[...], axis=0)
    pairs = 2.0 * TILE * 16
    loss_out[0] = jnp.sum(total[:8]) / pairs
    gs_out[0] = jnp.sum(total[8:]) / (pairs * sscale[0])
    for cp in sent:
        cp.wait_send()


def shards(*args):
    f32, bf16 = jnp.float32, jnp.bfloat16
    anyw = pl.BlockSpec(memory_space=pl.ANY)
    vmem = pl.BlockSpec(memory_space=pltpu.VMEM)
    smem = pl.BlockSpec(memory_space=pltpu.SMEM)
    sem = pltpu.SemaphoreType.DMA
    V = pltpu.VMEM
    return tuple(pl.pallas_call(
        kernel,
        out_shape=(
            jax.ShapeDtypeStruct((ROWS, SW), f32),
            jax.ShapeDtypeStruct((ROWS, SW), f32),
            jax.ShapeDtypeStruct((1,), f32),
            jax.ShapeDtypeStruct((1,), f32),
        ),
        in_specs=[anyw] * 4 + [smem] * 2,
        out_specs=(vmem, vmem, smem, smem),
        scratch_shapes=[
            V((TILE, W), bf16),
            V((NZ, 2, ROWS, W), bf16),
            V((TILE, TILE), f32),
            V((TILE, TILE), f32),
            V((TILE, TILE), f32),
            V((TILE, TILE), f32),
            V((TILE, TILE), f32),
            V((TILE, TILE), f32),
            V((TILE, TILE), bf16),
            V((2, 3, TILE, 128), f32),
            V((2, 3, TILE, 128), f32),
            V((2, 4, 8, TILE), f32),
            V((2, 4, 8, TILE), f32),
            V((16, 128), f32),
            V((16, 128), f32),
            V((16, 128), f32),
            V((16, 128), f32),
            V((16, 128), f32),
            V((16, 16, 128), f32),
            V((16, 16, 128), f32),
            V((ROWS, SW), f32),
            V((16, ROWS, SW), bf16),
            V((16, ROWS, SW), bf16),
            V((8, 2, ROWS, SW), f32),
            V((8, ROWS, SW), f32),
            V((ROWS, SW), f32),
            V((8, ROWS, SW), bf16),
            V((8, ROWS, SW), bf16),
            V((16, 128), f32),
            V((16, 16, 128), f32),
            V((16, 128), f32),
            V((16, 16, 128), f32),
            sem((6,)),
            sem((40,)), sem((40,)),
            sem((16,)), sem((16,)),
            sem((8,)), sem((8,)),
            sem((16,)), sem((16,)),
            sem((16,)), sem((16,)),
            sem((16,)), sem((16,)),
            sem((4,)), sem((4,)),
            sem((8,)), sem((8,)),
            sem((16,)), sem((16,)),
            sem((16,)), sem((16,)),
        ],
        compiler_params=pltpu.CompilerParams(
            collective_id=0, has_side_effects=True, vmem_limit_bytes=60 * 1024 * 1024
        ),
    )(*args))


def solution(mesh):
    return jax.shard_map(
        shards,
        mesh=mesh,
        in_specs=(
            P(("grp", "dev"), None),
            P(("grp", "dev"), None),
            P(("grp", "dev"), None),
            P(("grp", "dev"), None),
            P(),
            P(),
        ),
        out_specs=(P(("grp", "dev"), None), P(("grp", "dev"), None), P(), P()),
        check_vma=False,
    )
```

time: 92.1 us -> 77.9 us (0.85)
  Pallas kernels: 84.2 us -> 70 us
    pallas_call x1, Pallas kernels: 84.2 us -> 70 us  [shards(): pl.pallas_call(kernel, out_shape=(jax.ShapeDtypeStruct((ROWS, SW), f32),...]
where the time goes in v2:
time: 77.9 us; the launch traced here: 77.7 us
  Pallas kernels  70 us (90%)
  between operations  5.43 us (7%)
  local copies, waits for them, and re-layouts  2.26 us (3%)
    pallas_call x1, Pallas kernels, shards(): pl.pallas_call(kernel, out_shape=(jax.ShapeDtypeStruct((ROWS, SW), f32),...  70 us
    unnamed x4, local copies, waits for them, and re-layouts  2.26 us

profile of v2, /device:TPU:1, one launch (start us, length us, event | category | flops | bytes accessed | tf_op | source)
XLA Modules:
  0.0 77.7 jit_solution(9759769127839317776)
XLA Ops:
  1.9 70.0 %shard_map.93 = (f32[64,512]{1,0:T(8,128)}, f32[64,512]{1,0:T(8,128)}, f32[1]{0:T(128)}, f32[1]{0:T(128)}) custom-call(bf16[64,1280]{1,0:T(8,128)(2,1)} %ti.1, bf16[64,1280]{1,0:T(8,128)(2,1)} %tt.1, bf16[64,512]{1,0:T(8,128)(2,1)} %si.1, bf16[64,512]{1,0:T(8,128)(2,1)} %st.1, f32[1]{0:T(128)S(6)} %copy.14.tscale, f32[1]{0:T(128)S(6)} %copy.15.sscale), custom_call_target="tpu_custom_call" | custom-call | tf_op jit(solution)/shard_map/pallas_call | solution.py:483
  71.9 0.0 copy-start
  72.0 1.6 %copy.16 = f32[64,512]{1,0:T(8,128)} copy(f32[64,512]{1,0:T(8,128)} %get-tuple-element.8) | data formatting | bytes 262144
  73.6 0.0 copy-done
  73.6 0.7 copy.17
Async XLA Ops:
  71.9 1.6 %copy-start = (f32[64,512]{1,0:T(8,128)S(1)}, f32[64,512]{1,0:T(8,128)}, u32[]{:S(2)}) copy-start(f32[64,512]{1,0:T(8,128)} %get-tuple-element.9) | copy-start | bytes 393220

commit v3 on v2

--- a/solution.py
+++ b/solution.py
@@ -58,11 +58,11 @@
     gi_out, gt_out, loss_out, gs_out,
     img, txt, vt, vs, ert, ect, ers, ecs, wts,
     rmax, rsum, cmax, csum, rel, rst, cst, rall, call, rst_in, cst_in,
-    gi_own, gi_snd, gi_in, gt_all, gt_sib, gt_own, gt_snd, gt_in,
-    sc_snd, sc_a, sc_mid, sc_b,
+    gi_own, gi_mid, gi_snd, gi_in, g2_snd, g2_in, gt_all, gt_sib, gt_snd, gt_in,
+    sc_snd, sc_in,
     loc_sem, ps_s, ps_r, zs_s, zs_r, cs_s, cs_r,
-    rx_s, rx_r, cx_s, cx_r, gi_s, gi_r, sb_s, sb_r, gt_s, gt_r,
-    sa_s, sa_r, sb2_s, sb2_r,
+    rx_s, rx_r, cx_s, cx_r, g1_s, g1_r, g2_s, g2_r, sb_s, sb_r, gt_s, gt_r,
+    sc_s, sc_r,
 ):
     g, d = lax.axis_index("grp"), lax.axis_index("dev")
     x, y, z, c = g % 4, d // 4, ((d // 2) % 2) * 4 + g // 4, d % 2
@@ -294,11 +294,11 @@
     for h in range(2):
         for k in (1, 2, 3):
             t2_recv(h, k)
+    tile(3, 0, *LAST[0])
     for dz in (-3, 4):
         c_come(dz)
     tiles(0, 3, 2)
-    for strip, (c0, n) in enumerate(LAST):
-        tile(3, strip, c0, n)
+    tile(3, 1, *LAST[1])
 
     for part in range(2):
         high = jnp.max(cmax[part], axis=0)
@@ -374,37 +374,27 @@
             for s in range(3 if k < 6 else 2):
                 rmax[part, s, rows, :] = half * jnp.exp2(rmax[part, s, rows, :] - lse)
 
-    def pass2(strips):
-        def body(s, carry):
+    def pass2(c0, n, head, last, carry):
+        cols = pl.ds(c0, n)
+        k = n // 128
+
+        def body(s, carry, strip):
             loss_acc, scale_acc = carry
             rows = pl.ds(pl.multiple_of(s * 32, 32), 32)
             q = s // (CHUNK // 32)
-            for strip, (c0, n) in enumerate(strips):
-                cols = pl.ds(c0, n)
-                v = vs[rows, cols]
-                k = n // 128
-                teach = ert[rows, cols] * wide(rmax[0, strip, rows, :], k) + ect[rows, cols] * tall(cmax[0, q, :, cols], 4)
-                stud = ers[rows, cols] * wide(rmax[1, strip, rows, :], k) + ecs[rows, cols] * tall(cmax[1, q, :, cols], 4)
-                differ = stud - teach
-                wts[rows, cols] = differ.astype(jnp.bfloat16)
-                loss_acc = loss_acc + lanes(sublanes(teach * v, jnp.add), jnp.add)
-                scale_acc = scale_acc + lanes(sublanes(differ * v, jnp.add), jnp.add)
+            v = vs[rows, cols]
+            teach = ert[rows, cols] * wide(rmax[0, strip, rows, :], k) + ect[rows, cols] * tall(cmax[0, q, :, cols], 4)
+            stud = ers[rows, cols] * wide(rmax[1, strip, rows, :], k) + ecs[rows, cols] * tall(cmax[1, q, :, cols], 4)
+            differ = stud - teach
+            wts[rows, cols] = differ.astype(jnp.bfloat16)
+            loss_acc = loss_acc + lanes(sublanes(teach * v, jnp.add), jnp.add)
+            scale_acc = scale_acc + lanes(sublanes(differ * v, jnp.add), jnp.add)
             return loss_acc, scale_acc
 
-        return body
-
-    zero = jnp.zeros((8, 128), jnp.float32)
-    accs = lax.fori_loop(0, 24, pass2(STRIPS), (zero, zero), unroll=2)
-    loss_acc, scale_acc = lax.fori_loop(24, 32, pass2(LAST), accs, unroll=2)
-
-    back = LN2 / half
-    sc_snd[pl.ds(0, 8), :] = (row[8:, :] + col[8:, :]) * (LN2 / 16.0) - loss_acc * back
-    sc_snd[pl.ds(8, 8), :] = scale_acc * back
-    for dx, dy in plane:
-        i, dev = plane_peer(dx, dy)
-        send(sc_snd, sc_a.at[me_p], sa_s.at[i], sa_r.at[me_p], dev)
-
-    for q in (3, 2, 1, 0):
+        carry = lax.fori_loop(0, 24, functools.partial(body, strip=head), carry, unroll=4)
+        return lax.fori_loop(24, 32, functools.partial(body, strip=last), carry, unroll=4)
+
+    def text_parts(q):
         v = lax.dot_general(
             wts[:, 256 * q:256 * q + 256], img[:, TW:], TN, preferred_element_type=jnp.float32
         )
@@ -412,63 +402,163 @@
         gt_all[pair] = v.reshape(2, 2, ROWS, SW)
         send(gt_all.at[pair, sib], gt_sib.at[pair], sb_s.at[q], sb_r.at[q], other)
 
-    for q in range(4):
+    def text_both(q):
+        arrived(gt_sib.at[pl.ds(2 * q, 2)], sb_s.at[q], sb_r.at[q], other)
+
+    def own_part(dz, q):
+        rows = pl.ds(32 * q, 32)
+        return gt_all[SLOT[dz % 8], c, rows, :] + gt_sib[SLOT[dz % 8], rows, :]
+
+    def chain_ref(ref, sign, s, q):
+        return ref.at[s * 2 + (sign > 0), pl.ds(32 * q, 32)]
+
+    def chain_id(sign, s, q):
+        return (s * 2 + q) * 2 + (sign > 0)
+
+    def chain_wait(sign, s, q):
+        i = chain_id(sign, s, q)
+        arrived(chain_ref(gt_in, sign, s, q), gt_s.at[i], gt_r.at[i], up(-sign))
+        return chain_ref(gt_in, sign, s, q)[...].astype(jnp.float32)
+
+    def chain_send(sign, s, q):
+        v = own_part(sign * (3 - s), q)
+        if s > 0:
+            v = v + chain_wait(sign, s - 1, q)
+        chain_ref(gt_snd, sign, s, q)[...] = v.astype(jnp.bfloat16)
+        i = chain_id(sign, s, q)
+        send(chain_ref(gt_snd, sign, s, q), chain_ref(gt_in, sign, s, q), gt_s.at[i], gt_r.at[i], up(sign))
+
+    def far_send():
+        for q in range(2):
+            gt_snd[6, pl.ds(32 * q, 32)] = own_part(4, q).astype(jnp.bfloat16)
+        send(gt_snd.at[6], gt_in.at[6], gt_s.at[12], gt_r.at[12], up(4))
+
+    def far_wait():
+        arrived(gt_in.at[6], gt_s.at[12], gt_r.at[12], up(4))
+        return gt_in[6].astype(jnp.float32)
+
+    def image_parts(q):
         v = jnp.dot(
             wts[pl.ds(256 * q, 256), :], txt[:, :, :, TW:].reshape(TILE, SW), preferred_element_type=jnp.float32
         )
         for h, a, b, r in UNITS:
             if r // 256 == q:
                 o = r % 256
-                place = (b * 4 + a) if h == 0 else (a * 4 + b)
-                gi_snd[place, pl.ds(32 * h, 32), :] = v[o:o + 32].astype(jnp.bfloat16)
-                if place == 0:
-                    gi_own[pl.ds(32 * h, 32), :] = v[o:o + 32]
-    for dx, dy in plane:
-        i, dev = plane_peer(dx, dy)
-        send(gi_snd.at[dy * 4 + dx], gi_in.at[me_p], gi_s.at[i], gi_r.at[me_p], dev)
-
-    for q in (3, 2, 1, 0):
-        pair = pl.ds(2 * q, 2)
-        arrived(gt_sib.at[pair], sb_s.at[q], sb_r.at[q], other)
-        for dz in range(8):
-            k = SLOT[dz]
-            if k // 2 == q:
-                v = gt_all[k, c] + gt_sib[k]
-                if dz == 0:
-                    gt_own[...] = v
+                if b == 0:
+                    gi_own[h, a] = v[o:o + 32]
                 else:
-                    gt_snd[k] = v.astype(jnp.bfloat16)
-                    pz = (z + dz) % 8
-                    send(gt_snd.at[k], gt_in.at[z], gt_s.at[pz], gt_r.at[z], at(x, y, pz, c))
-
-    v = sc_snd[...]
-    for dx, dy in plane:
-        i, dev = plane_peer(dx, dy)
-        arrived(sc_a.at[i], sa_s.at[i], sa_r.at[i], dev)
-    sc_a[me_p] = v
-    sc_mid[...] = jnp.sum(sc_a[...], axis=0)
-    for dz, dc in column:
-        i, dev = column_peer(dz, dc)
-        send(sc_mid, sc_b.at[me_c], sb2_s.at[i], sb2_r.at[me_c], dev)
-
-    gi_out[...] = gi_own[...]
-    for dx, dy in plane:
-        i, dev = plane_peer(dx, dy)
-        arrived(gi_in.at[i], gi_s.at[i], gi_r.at[i], dev)
-        gi_out[...] += gi_in[i].astype(jnp.float32)
-    gt_out[...] = gt_own[...]
-    for dz in range(1, 8):
-        pz = (z + dz) % 8
-        arrived(gt_in.at[pz], gt_s.at[pz], gt_r.at[pz], at(x, y, pz, c))
-        gt_out[...] += gt_in[pz].astype(jnp.float32)
-    for dz, dc in column:
-        i, dev = column_peer(dz, dc)
-        arrived(sc_b.at[i], sb2_s.at[i], sb2_r.at[i], dev)
-    sc_b[me_c] = sc_mid[...]
-    total = jnp.sum(sc_b[...], axis=0)
+                    gi_snd[h, b, a] = v[o:o + 32].astype(jnp.bfloat16)
+
+    pieces = ((2, 2), (1, 1), (0, 1))
+
+    def stage1_id(h, b, p):
+        return (h * 4 + b) * 3 + p
+
+    def stage1_send(b, p):
+        for h in range(2):
+            i = stage1_id(h, 4 - b, p)
+            part = pl.ds(*pieces[p])
+            send(gi_snd.at[h, b, part], gi_in.at[h, 4 - b, part], g1_s.at[i], g1_r.at[i], along(h, 1, b))
+
+    def stage1_sum(h, p):
+        first_a, count = pieces[p]
+        for b in range(1, 4):
+            i = stage1_id(h, b, p)
+            arrived(gi_in.at[h, b, pl.ds(first_a, count)], g1_s.at[i], g1_r.at[i], along(h, 1, b))
+        for a in range(first_a, first_a + count):
+            v = gi_own[h, a] + gi_in[h, 1, a].astype(jnp.float32)
+            v = v + gi_in[h, 2, a].astype(jnp.float32) + gi_in[h, 3, a].astype(jnp.float32)
+            if a == 0:
+                gi_mid[h] = v
+            else:
+                g2_snd[h, a] = v.astype(jnp.bfloat16)
+                i = h * 4 + 4 - a
+                send(g2_snd.at[h, a], g2_in.at[h, 4 - a], g2_s.at[i], g2_r.at[i], along(h, 0, a))
+
+    def stage2_sum(h):
+        v = gi_mid[h]
+        for a in range(1, 4):
+            i = h * 4 + a
+            arrived(g2_in.at[h, a], g2_s.at[i], g2_r.at[i], along(h, 0, a))
+            v = v + g2_in[h, a].astype(jnp.float32)
+        gi_out[pl.ds(32 * h, 32), :] = v
+
+    def scalar_send(level, peers, peer, me):
+        for p in peers:
+            i, dev = peer(*p)
+            send(sc_snd.at[level], sc_in.at[level, me], sc_s.at[level, i], sc_r.at[level, me], dev)
+
+    def scalar_sum(level, peers, peer, me):
+        v = sc_snd[level]
+        for p in peers:
+            i, dev = peer(*p)
+            arrived(sc_in.at[level, i], sc_s.at[level, i], sc_r.at[level, i], dev)
+            v = v + sc_in[level, i]
+        return v
+
+    in_plane = (plane, plane_peer, me_p)
+    in_column = (column, column_peer, me_c)
+
+    zero = jnp.zeros((8, 128), jnp.float32)
+    accs = pass2(768, 256, 2, 1, (zero, zero))
+    text_parts(3)
+    accs = pass2(512, 256, 1, 1, accs)
+    text_parts(2)
+    loss_acc, scale_acc = pass2(0, 512, 0, 0, accs)
+
+    back = LN2 / half
+    loss_acc = (row[8:, :] + col[8:, :]) * (LN2 / 16.0) - loss_acc * back
+    sc_snd[0, pl.ds(0, 1), :] = jnp.sum(loss_acc, axis=0, keepdims=True)
+    sc_snd[0, pl.ds(1, 1), :] = jnp.sum(scale_acc * back, axis=0, keepdims=True)
+    scalar_send(0, *in_plane)
+
+    text_both(3)
+    for q in range(2):
+        chain_send(-1, 0, q)
+    image_parts(3)
+    for p in range(3):
+        stage1_send(2, p)
+    image_parts(1)
+    image_parts(2)
+    for p in range(3):
+        for b in (1, 3):
+            stage1_send(b, p)
+    text_both(2)
+    for q in range(2):
+        chain_send(1, 0, q)
+
+    text_parts(1)
+    text_parts(0)
+    image_parts(0)
+    sc_snd[1] = scalar_sum(0, *in_plane)
+    scalar_send(1, *in_column)
+    far_send()
+    text_both(1)
+    for q in range(2):
+        for sign in (-1, 1):
+            chain_send(sign, 1, q)
+    for h in range(2):
+        stage1_sum(h, 0)
+    text_both(0)
+    for q in range(2):
+        for sign in (-1, 1):
+            chain_send(sign, 2, q)
+    for h in range(2):
+        stage1_sum(h, 1)
+    far = far_wait()
+    for h in range(2):
+        stage1_sum(h, 2)
+    total = scalar_sum(1, *in_column)
+    for q in range(2):
+        v = own_part(0, q) + far[32 * q:32 * q + 32]
+        for sign in both:
+            v = v + chain_wait(sign, 2, q)
+        gt_out[pl.ds(32 * q, 32), :] = v
+    for h in range(2):
+        stage2_sum(h)
     pairs = 2.0 * TILE * 16
-    loss_out[0] = jnp.sum(total[:8]) / pairs
-    gs_out[0] = jnp.sum(total[8:]) / (pairs * sscale[0])
+    loss_out[0] = jnp.sum(total[:1]) / pairs
+    gs_out[0] = jnp.sum(total[1:]) / (pairs * sscale[0])
     for cp in sent:
         cp.wait_send()
 
@@ -511,29 +601,29 @@
             V((16, 128), f32),
             V((16, 16, 128), f32),
             V((16, 16, 128), f32),
-            V((ROWS, SW), f32),
-            V((16, ROWS, SW), bf16),
-            V((16, ROWS, SW), bf16),
+            V((2, 4, 32, SW), f32),
+            V((2, 32, SW), f32),
+            V((2, 4, 4, 32, SW), bf16),
+            V((2, 4, 4, 32, SW), bf16),
+            V((2, 4, 32, SW), bf16),
+            V((2, 4, 32, SW), bf16),
             V((8, 2, ROWS, SW), f32),
             V((8, ROWS, SW), f32),
-            V((ROWS, SW), f32),
             V((8, ROWS, SW), bf16),
             V((8, ROWS, SW), bf16),
-            V((16, 128), f32),
-            V((16, 16, 128), f32),
-            V((16, 128), f32),
-            V((16, 16, 128), f32),
+            V((2, 2, 128), f32),
+            V((2, 16, 2, 128), f32),
             sem((6,)),
             sem((40,)), sem((40,)),
             sem((16,)), sem((16,)),
             sem((8,)), sem((8,)),
             sem((16,)), sem((16,)),
             sem((16,)), sem((16,)),
+            sem((24,)), sem((24,)),
+            sem((8,)), sem((8,)),
+            sem((4,)), sem((4,)),
             sem((16,)), sem((16,)),
-            sem((4,)), sem((4,)),
-            sem((8,)), sem((8,)),
-            sem((16,)), sem((16,)),
-            sem((16,)), sem((16,)),
+            sem((2, 16)), sem((2, 16)),
         ],
         compiler_params=pltpu.CompilerParams(
             collective_id=0, has_side_effects=True, vmem_limit_bytes=60 * 1024 * 1024

time: 77.9 us -> 71.9 us (0.923); the launches traced: 77.7 us -> 70.7 us
  Pallas kernels: 70 us -> 63 us
    pallas_call x1, Pallas kernels: 70 us -> 63 us  [shards(): pl.pallas_call(kernel, out_shape=(jax.ShapeDtypeStruct((ROWS, SW), f32),...]
where the time goes in v3:
time: 71.9 us; the launch traced here: 70.7 us
  Pallas kernels  63 us (88%)
  between operations  5.43 us (8%)
  local copies, waits for them, and re-layouts  2.26 us (3%)
    pallas_call x1, Pallas kernels, shards(): pl.pallas_call(kernel, out_shape=(jax.ShapeDtypeStruct((ROWS, SW), f32),...  63 us
    unnamed x4, local copies, waits for them, and re-layouts  2.26 us

profile of v3, /device:TPU:1, one launch (start us, length us, event | category | flops | bytes accessed | tf_op | source)
XLA Modules:
  0.0 70.7 jit_solution(1836045270471494169)
XLA Ops:
  1.9 63.0 %shard_map.93 = (f32[64,512]{1,0:T(8,128)}, f32[64,512]{1,0:T(8,128)}, f32[1]{0:T(128)}, f32[1]{0:T(128)}) custom-call(bf16[64,1280]{1,0:T(8,128)(2,1)} %ti.1, bf16[64,1280]{1,0:T(8,128)(2,1)} %tt.1, bf16[64,512]{1,0:T(8,128)(2,1)} %si.1, bf16[64,512]{1,0:T(8,128)(2,1)} %st.1, f32[1]{0:T(128)S(6)} %copy.14.tscale, f32[1]{0:T(128)S(6)} %copy.15.sscale), custom_call_target="tpu_custom_call" | custom-call | tf_op jit(solution)/shard_map/pallas_call | solution.py:573
  65.0 0.0 copy-start
  65.0 1.6 %copy.16 = f32[64,512]{1,0:T(8,128)} copy(f32[64,512]{1,0:T(8,128)} %get-tuple-element.8) | data formatting | bytes 262144
  66.6 0.0 copy-done
  66.6 0.7 copy.17
Async XLA Ops:
  65.0 1.6 %copy-start = (f32[64,512]{1,0:T(8,128)S(1)}, f32[64,512]{1,0:T(8,128)}, u32[]{:S(2)}) copy-start(f32[64,512]{1,0:T(8,128)} %get-tuple-element.9) | copy-start | bytes 393220

commit v4 on v3

--- a/solution.py
+++ b/solution.py
@@ -55,7 +55,7 @@
 
 def kernel(
     ti, tt, si, st, tscale, sscale,
-    gi_out, gt_out, loss_out, gs_out,
+    gi_out, gt_out, sums_out,
     img, txt, vt, vs, ert, ect, ers, ecs, wts,
     rmax, rsum, cmax, csum, rel, rst, cst, rall, call, rst_in, cst_in,
     gi_own, gi_mid, gi_snd, gi_in, g2_snd, g2_in, gt_all, gt_sib, gt_snd, gt_in,
@@ -96,7 +96,7 @@
     local = []
 
     def bring(src, dst):
-        cp = pltpu.make_async_copy(src, dst, loc_sem.at[len(local)])
+        cp = pltpu.make_async_copy(src, dst, loc_sem)
         cp.start()
         local.append(cp)
 
@@ -111,71 +111,65 @@
     near = [along(0, axis, step) for axis in range(2) for step in (1, -1)] + [up(1), up(-1), other]
     for dev in near:
         pl.semaphore_signal(barrier, inc=1, device_id=dev, device_id_type=MESH)
-    for cp in local:
-        cp.wait()
+    pltpu.make_async_copy(img.at[pl.ds(0, 2 * ROWS)], img.at[pl.ds(0, 2 * ROWS)], loc_sem).wait()
     pl.semaphore_wait(barrier, len(near))
 
-    sent = []
-
-    def send(src, dst, ssem, rsem, dev):
-        cp = pltpu.make_async_remote_copy(
+    def remote(src, dst, ssem, rsem, dev):
+        return pltpu.make_async_remote_copy(
             src_ref=src, dst_ref=dst, send_sem=ssem, recv_sem=rsem, device_id=dev, device_id_type=MESH
         )
-        cp.start()
-        sent.append(cp)
-
-    def arrived(dst, ssem, rsem, dev):
-        pltpu.make_async_remote_copy(
-            src_ref=dst, dst_ref=dst, send_sem=ssem, recv_sem=rsem, device_id=dev, device_id_type=MESH
-        ).wait_recv()
+
+    def send(src, dst, ssem, rsem, dev):
+        remote(src, dst, ssem, rsem, dev).start()
+
+    def arrived(like, ssem, rsem):
+        remote(like, like, ssem, rsem, other).wait_recv()
+
+    def all_sent(like, ssem, rsem):
+        remote(like, like, ssem, rsem, other).wait_send()
 
     both = (1, -1)
 
     def unit(h, a, b, r0=0, n=32):
         return img.at[pl.ds(row_unit(h, a % 4, b % 4) + r0, n)]
 
-    def sem_id(h, stage, sign, k):
-        return 20 * h + (0, 2, 4, 12)[stage] + (sign > 0) + 2 * k
-
-    def psend(h, stage, sign, k, src, dst, axis):
-        i = sem_id(h, stage, sign, k)
-        send(src, dst, ps_s.at[i], ps_r.at[i], along(h, axis, sign))
-
-    def pwait(h, stage, sign, k, dst, axis):
-        i = sem_id(h, stage, sign, k)
-        arrived(dst, ps_s.at[i], ps_r.at[i], along(h, axis, -sign))
+    def psend(h, i, sign, src, dst, axis):
+        send(src, dst, ps_s, ps_r.at[i], along(h, axis, sign))
+
+    def pwait(i, n):
+        arrived(img.at[pl.ds(0, n)], ps_s, ps_r.at[i])
 
     def half_of(sign):
         return (0 if sign > 0 else 16), 16
 
-    def s1_send(h):
-        for sign in both:
-            psend(h, 0, sign, 0, unit(h, 0, 0), unit(h, -sign, 0), 0)
-
-    def s1_recv(h):
-        for sign in both:
-            pwait(h, 0, sign, 0, unit(h, -sign, 0), 0)
-            psend(h, 1, sign, 0, unit(h, -sign, 0, *half_of(sign)), unit(h, 2, 0, *half_of(sign)), 0)
-        for sign in both:
-            t1_send(h, 1 if sign > 0 else 2)
-
-    def s2_recv(h):
-        for sign in both:
-            pwait(h, 1, sign, 0, unit(h, 2, 0, *half_of(sign)), 0)
-        t1_send(h, 3)
-
-    def t1_send(h, k):
-        for sign in both:
-            psend(h, 2, sign, k, unit(h, A_OF[k], 0), unit(h, A_OF[k], -sign), 1)
-
-    def t1_recv(h, k):
-        for sign in both:
-            pwait(h, 2, sign, k, unit(h, A_OF[k], -sign), 1)
-            psend(h, 3, sign, k, unit(h, A_OF[k], -sign, *half_of(sign)), unit(h, A_OF[k], 2, *half_of(sign)), 1)
-
-    def t2_recv(h, k):
-        for sign in both:
-            pwait(h, 3, sign, k, unit(h, A_OF[k], 2, *half_of(sign)), 1)
+    hs = [(h, sign) for h in range(2) for sign in both]
+
+    def s1_send():
+        for h, sign in hs:
+            psend(h, 0, sign, unit(h, 0, 0), unit(h, -sign, 0), 0)
+
+    def s1_recv():
+        pwait(0, 128)
+        for h, sign in hs:
+            psend(h, 1, sign, unit(h, -sign, 0, *half_of(sign)), unit(h, 2, 0, *half_of(sign)), 0)
+        t1_send(1)
+        t1_send(2)
+
+    def s2_recv():
+        pwait(1, 64)
+        t1_send(3)
+
+    def t1_send(k):
+        for h, sign in hs:
+            psend(h, 2 + k, sign, unit(h, A_OF[k], 0), unit(h, A_OF[k], -sign), 1)
+
+    def t1_recv(k):
+        pwait(2 + k, 128)
+        for h, sign in hs:
+            psend(h, 6, sign, unit(h, A_OF[k], -sign, *half_of(sign)), unit(h, A_OF[k], 2, *half_of(sign)), 1)
+
+    def t2_recv():
+        pwait(6, 256)
 
     def zpart(dz, q):
         return txt.at[SLOT[dz % 8], c, pl.ds(32 * q, 32)]
@@ -183,26 +177,25 @@
     def first_half(sign):
         return 0 if sign > 0 else 1
 
-    def z_move(sign, s, q):
-        i = ((s - 1) * 2 + q) * 2 + (sign > 0)
-        send(zpart(-sign * (s - 1), q), zpart(-sign * s, q), zs_s.at[i], zs_r.at[i], up(sign))
-
-    def z_come(sign, s, q):
-        i = ((s - 1) * 2 + q) * 2 + (sign > 0)
-        arrived(zpart(-sign * s, q), zs_s.at[i], zs_r.at[i], up(-sign))
+    def z_move(sign, s, second):
+        q = first_half(sign) ^ second
+        send(zpart(-sign * (s - 1), q), zpart(-sign * s, q), zs_s, zs_r.at[(s - 1) * 2 + second], up(sign))
 
     def z_step(s, second):
+        arrived(txt.at[0, 0], zs_s, zs_r.at[(s - 1) * 2 + second])
         for sign in both:
-            q = first_half(sign) ^ second
-            z_come(sign, s, q)
-            if s < 3 or not second:
-                z_move(sign, s + 1, q)
+            if s < 3 or (s == 3 and not second):
+                z_move(sign, s + 1, second)
+
+    groups = ((0, 4), (4, 2), (6, 2))
 
     def c_move(dz):
-        send(txt.at[SLOT[dz % 8], c], txt.at[SLOT[dz % 8], c], cs_s.at[dz % 8], cs_r.at[dz % 8], other)
-
-    def c_come(dz):
-        arrived(txt.at[SLOT[dz % 8], sib], cs_s.at[dz % 8], cs_r.at[dz % 8], other)
+        k = SLOT[dz % 8]
+        i = (k >= 4) + (k >= 6)
+        send(txt.at[k, c], txt.at[k, c], cs_s, cs_r.at[i], other)
+
+    def c_come(i):
+        arrived(txt.at[pl.ds(*groups[i]), sib], cs_s, cs_r.at[i])
 
     lt, ls = tscale[0] * LOG2E, sscale[0] * LOG2E
     parts = ((0, TW, lt, vt, ert, ect), (TW, W, ls, vs, ers, ecs))
@@ -246,57 +239,41 @@
 
         lax.fori_loop(first, last, body, 0)
 
-    for h in range(2):
-        s1_send(h)
+    s1_send()
     for second in range(2):
         for sign in both:
-            z_move(sign, 1, first_half(sign) ^ second)
+            z_move(sign, 1, second)
     c_move(0)
-    for h in range(2):
-        t1_send(h, 0)
-    for h in range(2):
-        s1_recv(h)
+    t1_send(0)
+    s1_recv()
     z_step(1, 0)
-    for h in range(2):
-        t1_recv(h, 0)
+    t1_recv(0)
     z_step(1, 1)
     for sign in both:
         c_move(sign)
-    for h in range(2):
-        s2_recv(h)
+    s2_recv()
     z_step(2, 0)
-    for h in range(2):
-        t1_recv(h, 1)
+    t1_recv(1)
     z_step(2, 1)
     for sign in both:
         c_move(2 * sign)
-    for h in range(2):
-        t1_recv(h, 2)
-    for dz in (0, 1, -1, 2):
-        c_come(dz)
+    t1_recv(2)
+    c_come(0)
     tiles(0, 1, 0)
     z_step(3, 0)
-    for h in range(2):
-        t2_recv(h, 0)
     tiles(1, 2, 0)
-    for h in range(2):
-        t1_recv(h, 3)
+    t1_recv(3)
     z_step(3, 1)
     for sign in both:
         c_move(3 * sign)
     tiles(2, 3, 0)
-    for dz in (-2, 3):
-        c_come(dz)
+    c_come(1)
     tiles(0, 3, 1)
-    for sign in both:
-        z_come(sign, 4, first_half(sign))
+    z_step(4, 0)
     c_move(4)
-    for h in range(2):
-        for k in (1, 2, 3):
-            t2_recv(h, k)
+    t2_recv()
     tile(3, 0, *LAST[0])
-    for dz in (-3, 4):
-        c_come(dz)
+    c_come(2)
     tiles(0, 3, 2)
     tile(3, 1, *LAST[1])
 
@@ -310,7 +287,7 @@
             cst[pl.ds(part * 8 + (z + dz) % 8, 1), :] = lse[:, 128 * k:128 * k + 128]
     for dz, dc in column:
         i, dev = column_peer(dz, dc)
-        send(cst, cst_in.at[me_c], cx_s.at[i], cx_r.at[me_c], dev)
+        send(cst, cst_in.at[me_c], cx_s, cx_r, dev)
 
     for part in range(2):
         for k in range(8):
@@ -334,7 +311,7 @@
                 rst[pl.ds(part * 8 + h * 4 + (b + (y, x)[h]) % 4, 1), :] = v[h][k:k + 1]
     for dx, dy in plane:
         i, dev = plane_peer(dx, dy)
-        send(rst, rst_in.at[me_p], rx_s.at[i], rx_r.at[me_p], dev)
+        send(rst, rst_in.at[me_p], rx_s, rx_r, dev)
     cst_in[me_c] = cst[...]
     rst_in[me_p] = rst[...]
 
@@ -343,9 +320,7 @@
         return m + jnp.log2(jnp.sum(jnp.exp2(v - m[None]), axis=0))
 
     half = 0.5 * sscale[0]
-    for dz, dc in column:
-        i, dev = column_peer(dz, dc)
-        arrived(cst_in.at[i], cx_s.at[i], cx_r.at[i], dev)
+    arrived(cst_in.at[pl.ds(0, 15)], cx_s, cx_r)
     col = total_lse(cst_in[...])
     call[...] = col
     for part in range(2):
@@ -353,9 +328,7 @@
         for dz in range(8):
             lse[SLOT[dz]] = call[pl.ds(part * 8 + (z + dz) % 8, 1), :]
         cmax[part] = half * jnp.exp2(cmax[part] - jnp.concatenate(lse, axis=1)[None])
-    for dx, dy in plane:
-        i, dev = plane_peer(dx, dy)
-        arrived(rst_in.at[i], rx_s.at[i], rx_r.at[i], dev)
+    arrived(rst_in.at[pl.ds(0, 15)], rx_s, rx_r)
     row = total_lse(rst_in[...])
     rall[...] = row
     for part in range(2):
@@ -400,10 +373,10 @@
         )
         pair = pl.ds(2 * q, 2)
         gt_all[pair] = v.reshape(2, 2, ROWS, SW)
-        send(gt_all.at[pair, sib], gt_sib.at[pair], sb_s.at[q], sb_r.at[q], other)
+        send(gt_all.at[pair, sib], gt_sib.at[pair], sb_s, sb_r.at[q], other)
 
     def text_both(q):
-        arrived(gt_sib.at[pl.ds(2 * q, 2)], sb_s.at[q], sb_r.at[q], other)
+        arrived(gt_sib.at[pl.ds(2 * q, 2)], sb_s, sb_r.at[q])
 
     def own_part(dz, q):
         rows = pl.ds(32 * q, 32)
@@ -412,30 +385,29 @@
     def chain_ref(ref, sign, s, q):
         return ref.at[s * 2 + (sign > 0), pl.ds(32 * q, 32)]
 
-    def chain_id(sign, s, q):
-        return (s * 2 + q) * 2 + (sign > 0)
-
-    def chain_wait(sign, s, q):
-        i = chain_id(sign, s, q)
-        arrived(chain_ref(gt_in, sign, s, q), gt_s.at[i], gt_r.at[i], up(-sign))
+    def chain_wait(s, q):
+        arrived(gt_in.at[0], gt_s, gt_r.at[s * 2 + q])
+
+    def chain_part(sign, s, q):
         return chain_ref(gt_in, sign, s, q)[...].astype(jnp.float32)
 
     def chain_send(sign, s, q):
         v = own_part(sign * (3 - s), q)
         if s > 0:
-            v = v + chain_wait(sign, s - 1, q)
+            v = v + chain_part(sign, s - 1, q)
         chain_ref(gt_snd, sign, s, q)[...] = v.astype(jnp.bfloat16)
-        i = chain_id(sign, s, q)
-        send(chain_ref(gt_snd, sign, s, q), chain_ref(gt_in, sign, s, q), gt_s.at[i], gt_r.at[i], up(sign))
+        send(chain_ref(gt_snd, sign, s, q), chain_ref(gt_in, sign, s, q), gt_s, gt_r.at[s * 2 + q], up(sign))
+
+    def chain_step(s):
+        for q in range(2):
+            chain_wait(s - 1, q)
+            for sign in both:
+                chain_send(sign, s, q)
 
     def far_send():
         for q in range(2):
             gt_snd[6, pl.ds(32 * q, 32)] = own_part(4, q).astype(jnp.bfloat16)
-        send(gt_snd.at[6], gt_in.at[6], gt_s.at[12], gt_r.at[12], up(4))
-
-    def far_wait():
-        arrived(gt_in.at[6], gt_s.at[12], gt_r.at[12], up(4))
-        return gt_in[6].astype(jnp.float32)
+        send(gt_snd.at[6], gt_in.at[6], gt_s, gt_r.at[6], up(4))
 
     def image_parts(q):
         v = jnp.dot(
@@ -451,20 +423,14 @@
 
     pieces = ((2, 2), (1, 1), (0, 1))
 
-    def stage1_id(h, b, p):
-        return (h * 4 + b) * 3 + p
-
     def stage1_send(b, p):
         for h in range(2):
-            i = stage1_id(h, 4 - b, p)
             part = pl.ds(*pieces[p])
-            send(gi_snd.at[h, b, part], gi_in.at[h, 4 - b, part], g1_s.at[i], g1_r.at[i], along(h, 1, b))
+            send(gi_snd.at[h, b, part], gi_in.at[h, 4 - b, part], g1_s, g1_r.at[h * 3 + p], along(h, 1, b))
 
     def stage1_sum(h, p):
         first_a, count = pieces[p]
-        for b in range(1, 4):
-            i = stage1_id(h, b, p)
-            arrived(gi_in.at[h, b, pl.ds(first_a, count)], g1_s.at[i], g1_r.at[i], along(h, 1, b))
+        arrived(gi_in.at[h, pl.ds(1, 3), pl.ds(first_a, count)], g1_s, g1_r.at[h * 3 + p])
         for a in range(first_a, first_a + count):
             v = gi_own[h, a] + gi_in[h, 1, a].astype(jnp.float32)
             v = v + gi_in[h, 2, a].astype(jnp.float32) + gi_in[h, 3, a].astype(jnp.float32)
@@ -472,29 +438,24 @@
                 gi_mid[h] = v
             else:
                 g2_snd[h, a] = v.astype(jnp.bfloat16)
-                i = h * 4 + 4 - a
-                send(g2_snd.at[h, a], g2_in.at[h, 4 - a], g2_s.at[i], g2_r.at[i], along(h, 0, a))
+                send(g2_snd.at[h, a], g2_in.at[h, 4 - a], g2_s, g2_r.at[h], along(h, 0, a))
 
     def stage2_sum(h):
+        arrived(g2_in.at[h, pl.ds(1, 3)], g2_s, g2_r.at[h])
         v = gi_mid[h]
         for a in range(1, 4):
-            i = h * 4 + a
-            arrived(g2_in.at[h, a], g2_s.at[i], g2_r.at[i], along(h, 0, a))
             v = v + g2_in[h, a].astype(jnp.float32)
         gi_out[pl.ds(32 * h, 32), :] = v
 
     def scalar_send(level, peers, peer, me):
         for p in peers:
             i, dev = peer(*p)
-            send(sc_snd.at[level], sc_in.at[level, me], sc_s.at[level, i], sc_r.at[level, me], dev)
-
-    def scalar_sum(level, peers, peer, me):
-        v = sc_snd[level]
-        for p in peers:
-            i, dev = peer(*p)
-            arrived(sc_in.at[level, i], sc_s.at[level, i], sc_r.at[level, i], dev)
-            v = v + sc_in[level, i]
-        return v
+            send(sc_snd.at[level], sc_in.at[level, me], sc_s, sc_r.at[level], dev)
+
+    def scalar_sum(level, me):
+        arrived(sc_in.at[level, pl.ds(0, 15)], sc_s, sc_r.at[level])
+        sc_in[level, me] = sc_snd[level]
+        return jnp.sum(sc_in[level], axis=0)
 
     in_plane = (plane, plane_peer, me_p)
     in_column = (column, column_peer, me_c)
@@ -530,37 +491,48 @@
     text_parts(1)
     text_parts(0)
     image_parts(0)
-    sc_snd[1] = scalar_sum(0, *in_plane)
+    sc_snd[1] = scalar_sum(0, me_p)
     scalar_send(1, *in_column)
     far_send()
     text_both(1)
-    for q in range(2):
-        for sign in (-1, 1):
-            chain_send(sign, 1, q)
+    chain_step(1)
     for h in range(2):
         stage1_sum(h, 0)
     text_both(0)
-    for q in range(2):
-        for sign in (-1, 1):
-            chain_send(sign, 2, q)
+    chain_step(2)
     for h in range(2):
         stage1_sum(h, 1)
-    far = far_wait()
+    arrived(gt_in.at[6], gt_s, gt_r.at[6])
     for h in range(2):
         stage1_sum(h, 2)
-    total = scalar_sum(1, *in_column)
+    total = scalar_sum(1, me_c)
     for q in range(2):
-        v = own_part(0, q) + far[32 * q:32 * q + 32]
-        for sign in both:
-            v = v + chain_wait(sign, 2, q)
-        gt_out[pl.ds(32 * q, 32), :] = v
+        rows = pl.ds(32 * q, 32)
+        chain_wait(2, q)
+        v = own_part(0, q) + gt_in[6, rows, :].astype(jnp.float32)
+        gt_out[rows, :] = v + chain_part(1, 2, q) + chain_part(-1, 2, q)
     for h in range(2):
         stage2_sum(h)
     pairs = 2.0 * TILE * 16
-    loss_out[0] = jnp.sum(total[:1]) / pairs
-    gs_out[0] = jnp.sum(total[1:]) / (pairs * sscale[0])
-    for cp in sent:
-        cp.wait_send()
+    sums_out[pl.ds(0, 1), :] = total[:1] / pairs
+    sums_out[pl.ds(1, 1), :] = total[1:] / (pairs * sscale[0])
+    all_sent(img.at[pl.ds(0, 960)], ps_s, ps_r.at[0])
+    all_sent(txt.at[pl.ds(0, 7), 0], zs_s, zs_r.at[0])
+    all_sent(txt.at[:, 0], cs_s, cs_r.at[0])
+    all_sent(rst_in.at[pl.ds(0, 15)], rx_s, rx_r)
+    all_sent(cst_in.at[pl.ds(0, 15)], cx_s, cx_r)
+    all_sent(gi_in.at[:, pl.ds(0, 3)], g1_s, g1_r.at[0])
+    all_sent(g2_in.at[:, pl.ds(0, 3)], g2_s, g2_r.at[0])
+    all_sent(gt_sib, sb_s, sb_r.at[0])
+    all_sent(gt_in.at[pl.ds(0, 7)], gt_s, gt_r.at[0])
+    all_sent(sc_in.at[:, pl.ds(0, 15)], sc_s, sc_r.at[0])
+
+
+def finish(gi, gt, sums, gi_out, gt_out, loss_out, gs_out):
+    gi_out[...] = gi[...]
+    gt_out[...] = gt[...]
+    loss_out[0] = jnp.sum(sums[pl.ds(0, 1), :])
+    gs_out[0] = jnp.sum(sums[pl.ds(1, 1), :])
 
 
 def shards(*args):
@@ -570,16 +542,13 @@
     smem = pl.BlockSpec(memory_space=pltpu.SMEM)
     sem = pltpu.SemaphoreType.DMA
     V = pltpu.VMEM
-    return tuple(pl.pallas_call(
+    rows = jax.ShapeDtypeStruct((ROWS, SW), f32)
+    one = jax.ShapeDtypeStruct((1,), f32)
+    sums = pl.pallas_call(
         kernel,
-        out_shape=(
-            jax.ShapeDtypeStruct((ROWS, SW), f32),
-            jax.ShapeDtypeStruct((ROWS, SW), f32),
-            jax.ShapeDtypeStruct((1,), f32),
-            jax.ShapeDtypeStruct((1,), f32),
-        ),
+        out_shape=(rows, rows, jax.ShapeDtypeStruct((2, 128), f32)),
         in_specs=[anyw] * 4 + [smem] * 2,
-        out_specs=(vmem, vmem, smem, smem),
+        out_specs=(vmem, vmem, vmem),
         scratch_shapes=[
             V((TILE, W), bf16),
             V((NZ, 2, ROWS, W), bf16),
@@ -613,22 +582,28 @@
             V((8, ROWS, SW), bf16),
             V((2, 2, 128), f32),
             V((2, 16, 2, 128), f32),
-            sem((6,)),
-            sem((40,)), sem((40,)),
-            sem((16,)), sem((16,)),
-            sem((8,)), sem((8,)),
-            sem((16,)), sem((16,)),
-            sem((16,)), sem((16,)),
-            sem((24,)), sem((24,)),
-            sem((8,)), sem((8,)),
-            sem((4,)), sem((4,)),
-            sem((16,)), sem((16,)),
-            sem((2, 16)), sem((2, 16)),
+            sem,
+            sem, sem((7,)),
+            sem, sem((7,)),
+            sem, sem((3,)),
+            sem, sem,
+            sem, sem,
+            sem, sem((6,)),
+            sem, sem((2,)),
+            sem, sem((4,)),
+            sem, sem((7,)),
+            sem, sem((2,)),
         ],
         compiler_params=pltpu.CompilerParams(
             collective_id=0, has_side_effects=True, vmem_limit_bytes=60 * 1024 * 1024
         ),
-    )(*args))
+    )(*args)
+    return tuple(pl.pallas_call(
+        finish,
+        out_shape=(rows, rows, one, one),
+        in_specs=[vmem] * 3,
+        out_specs=(vmem, vmem, smem, smem),
+    )(*sums))
 
 
 def solution(mesh):

time: 71.9 us -> 62.2 us (0.87)
  Pallas kernels: 63 us -> 59.2 us
  between operations: 5.43 us -> 1.93 us
  local copies, waits for them, and re-layouts: 2.26 us -> 0 us
    pallas_call x1 -> x2, Pallas kernels: 63 us -> 59.2 us  [the longest x1 57.5 us: shards(): pl.pallas_call(kernel, out_shape=(rows, rows, jax.ShapeDtypeStruct((2, 12...]
    unnamed x4 -> x0, local copies, waits for them, and re-layouts: 2.26 us -> none
where the time goes in v4:
time: 62.2 us; the launch traced here: 61.2 us
  Pallas kernels  59.2 us (95%)
  between operations  1.93 us (3%)
    pallas_call x1, Pallas kernels, shards(): pl.pallas_call(kernel, out_shape=(rows, rows, jax.ShapeDtypeStruct((2, 12...  57.5 us
    pallas_call x1, Pallas kernels, shards(): pl.pallas_call(finish, out_shape=(rows, rows, one, one), in_specs=[vmem]...  1.69 us

profile of v4, /device:TPU:1, one launch (start us, length us, event | category | flops | bytes accessed | tf_op | source)
XLA Modules:
  0.0 61.2 jit_solution(4152651463043914813)
XLA Ops:
  1.9 57.5 %shard_map.93 = (f32[64,512]{1,0:T(8,128)}, f32[64,512]{1,0:T(8,128)}, f32[2,128]{1,0:T(2,128)}) custom-call(bf16[64,1280]{1,0:T(8,128)(2,1)} %ti.1, bf16[64,1280]{1,0:T(8,128)(2,1)} %tt.1, bf16[64,512]{1,0:T(8,128)(2,1)} %si.1, bf16[64,512]{1,0:T(8,128)(2,1)} %st.1, f32[1]{0:T(128)S(6)} %copy.10.tscale, f32[1]{0:T(128)S(6)} %copy.11.sscale), custom_call_target="tpu_custom_call" | custom-call | tf_op jit(solution)/shard_map/pallas_call | solution.py:547
  59.5 1.7 %shard_map.94 = (f32[64,512]{1,0:T(8,128)}, f32[64,512]{1,0:T(8,128)}, f32[1]{0:T(128)}, f32[1]{0:T(128)}) custom-call(f32[64,512]{1,0:T(8,128)} %get-tuple-element.7.gi, f32[64,512]{1,0:T(8,128)} %get-tuple-element.8.gt, f32[2,128]{1,0:T(2,128)} %get-tuple-element.9.sums), custom_call_target="tpu_custom_call" | custom-call | tf_op jit(solution)/shard_map/pallas_call | solution.py:601

commit v5 on v4

--- a/solution.py
+++ b/solution.py
@@ -347,36 +347,40 @@
             for s in range(3 if k < 6 else 2):
                 rmax[part, s, rows, :] = half * jnp.exp2(rmax[part, s, rows, :] - lse)
 
-    def pass2(c0, n, head, last, carry):
-        cols = pl.ds(c0, n)
-        k = n // 128
-
-        def body(s, carry, strip):
+    def pass2(pieces, carry):
+        def body(s, carry, group):
             loss_acc, scale_acc = carry
             rows = pl.ds(pl.multiple_of(s * 32, 32), 32)
             q = s // (CHUNK // 32)
-            v = vs[rows, cols]
-            teach = ert[rows, cols] * wide(rmax[0, strip, rows, :], k) + ect[rows, cols] * tall(cmax[0, q, :, cols], 4)
-            stud = ers[rows, cols] * wide(rmax[1, strip, rows, :], k) + ecs[rows, cols] * tall(cmax[1, q, :, cols], 4)
-            differ = stud - teach
-            wts[rows, cols] = differ.astype(jnp.bfloat16)
-            loss_acc = loss_acc + lanes(sublanes(teach * v, jnp.add), jnp.add)
-            scale_acc = scale_acc + lanes(sublanes(differ * v, jnp.add), jnp.add)
+            for c0, n, *strips in pieces:
+                cols = pl.ds(c0, n)
+                k = n // 128
+                strip = strips[group]
+                v = vs[rows, cols]
+                teach = ert[rows, cols] * wide(rmax[0, strip, rows, :], k) + ect[rows, cols] * tall(cmax[0, q, :, cols], 4)
+                stud = ers[rows, cols] * wide(rmax[1, strip, rows, :], k) + ecs[rows, cols] * tall(cmax[1, q, :, cols], 4)
+                differ = stud - teach
+                wts[rows, cols] = differ.astype(jnp.bfloat16)
+                loss_acc = loss_acc + lanes(sublanes(teach * v, jnp.add), jnp.add)
+                scale_acc = scale_acc + lanes(sublanes(differ * v, jnp.add), jnp.add)
             return loss_acc, scale_acc
 
-        carry = lax.fori_loop(0, 24, functools.partial(body, strip=head), carry, unroll=4)
-        return lax.fori_loop(24, 32, functools.partial(body, strip=last), carry, unroll=4)
-
-    def text_parts(q):
+        carry = lax.fori_loop(0, 24, functools.partial(body, group=0), carry, unroll=2)
+        return lax.fori_loop(24, 32, functools.partial(body, group=1), carry, unroll=2)
+
+    slots = ((5, 3), (3, 2), (1, 2), (0, 1))
+
+    def text_parts(i):
+        k, n = slots[i]
         v = lax.dot_general(
-            wts[:, 256 * q:256 * q + 256], img[:, TW:], TN, preferred_element_type=jnp.float32
+            wts[:, 128 * k:128 * (k + n)], img[:, TW:], TN, preferred_element_type=jnp.float32
         )
-        pair = pl.ds(2 * q, 2)
-        gt_all[pair] = v.reshape(2, 2, ROWS, SW)
-        send(gt_all.at[pair, sib], gt_sib.at[pair], sb_s, sb_r.at[q], other)
-
-    def text_both(q):
-        arrived(gt_sib.at[pl.ds(2 * q, 2)], sb_s, sb_r.at[q])
+        some = pl.ds(k, n)
+        gt_all[some] = v.reshape(n, 2, ROWS, SW)
+        send(gt_all.at[some, sib], gt_sib.at[some], sb_s, sb_r.at[i], other)
+
+    def text_both(i):
+        arrived(gt_sib.at[pl.ds(*slots[i])], sb_s, sb_r.at[i])
 
     def own_part(dz, q):
         rows = pl.ds(32 * q, 32)
@@ -385,29 +389,28 @@
     def chain_ref(ref, sign, s, q):
         return ref.at[s * 2 + (sign > 0), pl.ds(32 * q, 32)]
 
-    def chain_wait(s, q):
-        arrived(gt_in.at[0], gt_s, gt_r.at[s * 2 + q])
+    def chain_wait(s, second):
+        arrived(gt_in.at[0], gt_s, gt_r.at[s * 2 + second])
 
     def chain_part(sign, s, q):
         return chain_ref(gt_in, sign, s, q)[...].astype(jnp.float32)
 
-    def chain_send(sign, s, q):
-        v = own_part(sign * (3 - s), q)
-        if s > 0:
-            v = v + chain_part(sign, s - 1, q)
-        chain_ref(gt_snd, sign, s, q)[...] = v.astype(jnp.bfloat16)
-        send(chain_ref(gt_snd, sign, s, q), chain_ref(gt_in, sign, s, q), gt_s, gt_r.at[s * 2 + q], up(sign))
-
-    def chain_step(s):
-        for q in range(2):
-            chain_wait(s - 1, q)
-            for sign in both:
-                chain_send(sign, s, q)
+    def chain_send(s, second):
+        for sign in both:
+            q = first_half(sign) ^ second
+            v = own_part(sign * (3 - s), q)
+            if s > 0:
+                v = v + chain_part(sign, s - 1, q)
+            if s == 1 and not second:
+                v = v + gt_in[6, pl.ds(32 * q, 32), :].astype(jnp.float32)
+            chain_ref(gt_snd, sign, s, q)[...] = v.astype(jnp.bfloat16)
+            send(chain_ref(gt_snd, sign, s, q), chain_ref(gt_in, sign, s, q), gt_s, gt_r.at[s * 2 + second], up(sign))
 
     def far_send():
-        for q in range(2):
-            gt_snd[6, pl.ds(32 * q, 32)] = own_part(4, q).astype(jnp.bfloat16)
-        send(gt_snd.at[6], gt_in.at[6], gt_s, gt_r.at[6], up(4))
+        for sign in both:
+            rows = pl.ds(32 * first_half(sign), 32)
+            gt_snd[6, rows] = own_part(4, first_half(sign)).astype(jnp.bfloat16)
+            send(gt_snd.at[6, rows], gt_in.at[6, rows], gt_s, gt_r.at[6], up(2 * sign))
 
     def image_parts(q):
         v = jnp.dot(
@@ -461,11 +464,9 @@
     in_column = (column, column_peer, me_c)
 
     zero = jnp.zeros((8, 128), jnp.float32)
-    accs = pass2(768, 256, 2, 1, (zero, zero))
-    text_parts(3)
-    accs = pass2(512, 256, 1, 1, accs)
-    text_parts(2)
-    loss_acc, scale_acc = pass2(0, 512, 0, 0, accs)
+    accs = pass2(((640, 128, 1, 1), (768, 256, 2, 1)), (zero, zero))
+    text_parts(0)
+    loss_acc, scale_acc = pass2(((512, 128, 1, 1), (0, 512, 0, 0)), accs)
 
     back = LN2 / half
     loss_acc = (row[8:, :] + col[8:, :]) * (LN2 / 16.0) - loss_acc * back
@@ -473,44 +474,43 @@
     sc_snd[0, pl.ds(1, 1), :] = jnp.sum(scale_acc * back, axis=0, keepdims=True)
     scalar_send(0, *in_plane)
 
-    text_both(3)
-    for q in range(2):
-        chain_send(-1, 0, q)
-    image_parts(3)
+    text_both(0)
+    far_send()
+    chain_send(0, 1)
+    chain_send(0, 0)
+    text_parts(1)
+    for q in (3, 1, 2):
+        image_parts(q)
     for p in range(3):
-        stage1_send(2, p)
-    image_parts(1)
-    image_parts(2)
-    for p in range(3):
-        for b in (1, 3):
+        for b in (2, 1, 3):
             stage1_send(b, p)
-    text_both(2)
-    for q in range(2):
-        chain_send(1, 0, q)
-
-    text_parts(1)
-    text_parts(0)
+    text_parts(2)
+    text_both(1)
+    chain_wait(0, 1)
+    chain_send(1, 1)
+    chain_wait(0, 0)
+    arrived(gt_in.at[6], gt_s, gt_r.at[6])
+    chain_send(1, 0)
     image_parts(0)
+    text_parts(3)
     sc_snd[1] = scalar_sum(0, me_p)
     scalar_send(1, *in_column)
-    far_send()
-    text_both(1)
-    chain_step(1)
     for h in range(2):
         stage1_sum(h, 0)
-    text_both(0)
-    chain_step(2)
+    text_both(2)
+    for second in (1, 0):
+        chain_wait(1, second)
+        chain_send(2, second)
     for h in range(2):
         stage1_sum(h, 1)
-    arrived(gt_in.at[6], gt_s, gt_r.at[6])
     for h in range(2):
         stage1_sum(h, 2)
+    text_both(3)
     total = scalar_sum(1, me_c)
+    for second in (1, 0):
+        chain_wait(2, second)
     for q in range(2):
-        rows = pl.ds(32 * q, 32)
-        chain_wait(2, q)
-        v = own_part(0, q) + gt_in[6, rows, :].astype(jnp.float32)
-        gt_out[rows, :] = v + chain_part(1, 2, q) + chain_part(-1, 2, q)
+        gt_out[pl.ds(32 * q, 32), :] = own_part(0, q) + chain_part(1, 2, q) + chain_part(-1, 2, q)
     for h in range(2):
         stage2_sum(h)
     pairs = 2.0 * TILE * 16

time: 62.2 us -> 60.8 us (0.977); the launches traced: 61.2 us -> 60.7 us
  no operation moved by 1% of the time
where the time goes in v5:
time: 60.8 us; the launch traced here: 60.7 us
  Pallas kernels  58.7 us (97%)
  between operations  1.93 us (3%)
    pallas_call x1, Pallas kernels, shards(): pl.pallas_call(kernel, out_shape=(rows, rows, jax.ShapeDtypeStruct((2, 12...  57 us
    pallas_call x1, Pallas kernels, shards(): pl.pallas_call(finish, out_shape=(rows, rows, one, one), in_specs=[vmem]...  1.69 us

profile of v5, /device:TPU:1, one launch (start us, length us, event | category | flops | bytes accessed | tf_op | source)
XLA Modules:
  0.0 60.7 jit_solution(3726158031122236507)
XLA Ops:
  1.9 57.0 %shard_map.93 = (f32[64,512]{1,0:T(8,128)}, f32[64,512]{1,0:T(8,128)}, f32[2,128]{1,0:T(2,128)}) custom-call(bf16[64,1280]{1,0:T(8,128)(2,1)} %ti.1, bf16[64,1280]{1,0:T(8,128)(2,1)} %tt.1, bf16[64,512]{1,0:T(8,128)(2,1)} %si.1, bf16[64,512]{1,0:T(8,128)(2,1)} %st.1, f32[1]{0:T(128)S(6)} %copy.10.tscale, f32[1]{0:T(128)S(6)} %copy.11.sscale), custom_call_target="tpu_custom_call" | custom-call | tf_op jit(solution)/shard_map/pallas_call | solution.py:547
  59.0 1.7 %shard_map.94 = (f32[64,512]{1,0:T(8,128)}, f32[64,512]{1,0:T(8,128)}, f32[1]{0:T(128)}, f32[1]{0:T(128)}) custom-call(f32[64,512]{1,0:T(8,128)} %get-tuple-element.7.gi, f32[64,512]{1,0:T(8,128)} %get-tuple-element.8.gt, f32[2,128]{1,0:T(2,128)} %get-tuple-element.9.sums), custom_call_target="tpu_custom_call" | custom-call | tf_op jit(solution)/shard_map/pallas_call | solution.py:601

commit v6 on v5

--- a/solution.py
+++ b/solution.py
@@ -55,7 +55,7 @@
 
 def kernel(
     ti, tt, si, st, tscale, sscale,
-    gi_out, gt_out, sums_out,
+    out,
     img, txt, vt, vs, ert, ect, ers, ecs, wts,
     rmax, rsum, cmax, csum, rel, rst, cst, rall, call, rst_in, cst_in,
     gi_own, gi_mid, gi_snd, gi_in, g2_snd, g2_in, gt_all, gt_sib, gt_snd, gt_in,
@@ -200,37 +200,39 @@
     lt, ls = tscale[0] * LOG2E, sscale[0] * LOG2E
     parts = ((0, TW, lt, vt, ert, ect), (TW, W, ls, vs, ers, ecs))
 
-    def tile(q, strip, c0, n):
-        r0 = q * CHUNK
+    def tile(q, strip, c0, n, count=1):
         cols = pl.ds(c0, n)
         blocks = pl.ds(c0 // 128, n // 128)
         for part, (lo, hi, scale, raw, er, ec) in enumerate(parts):
-            raw[pl.ds(r0, CHUNK), cols] = scale * lax.dot_general(
-                img[pl.ds(r0, CHUNK), lo:hi],
+            all_rows = pl.ds(q * CHUNK, count * CHUNK)
+            raw[all_rows, cols] = scale * lax.dot_general(
+                img[all_rows, lo:hi],
                 txt[blocks, :, :, lo:hi].reshape(n, hi - lo),
                 NT,
                 preferred_element_type=jnp.float32,
             )
-            peak = None
-            for s in range(CHUNK // 32):
-                rows = pl.ds(r0 + 32 * s, 32)
-                v = raw[rows, cols]
-                m = lanes(v, jnp.maximum)
-                e = jnp.exp2(v - wide(m, n // 128))
-                er[rows, cols] = e
-                rmax[part, strip, rows, :] = m
-                rsum[part, strip, rows, :] = lanes(e, jnp.add)
-                high = sublanes(v, jnp.maximum)
-                peak = high if peak is None else jnp.maximum(peak, high)
-            total = None
-            for s in range(CHUNK // 32):
-                rows = pl.ds(r0 + 32 * s, 32)
-                e = jnp.exp2(raw[rows, cols] - tall(peak, 4))
-                ec[rows, cols] = e
-                add = sublanes(e, jnp.add)
-                total = add if total is None else total + add
-            cmax[part, q, :, cols] = peak
-            csum[part, q, :, cols] = total
+            for g in range(count):
+                r0 = (q + g) * CHUNK
+                peak = None
+                for s in range(CHUNK // 32):
+                    rows = pl.ds(r0 + 32 * s, 32)
+                    v = raw[rows, cols]
+                    m = lanes(v, jnp.maximum)
+                    e = jnp.exp2(v - wide(m, n // 128))
+                    er[rows, cols] = e
+                    rmax[part, strip, rows, :] = m
+                    rsum[part, strip, rows, :] = lanes(e, jnp.add)
+                    high = sublanes(v, jnp.maximum)
+                    peak = high if peak is None else jnp.maximum(peak, high)
+                total = None
+                for s in range(CHUNK // 32):
+                    rows = pl.ds(r0 + 32 * s, 32)
+                    e = jnp.exp2(raw[rows, cols] - tall(peak, 4))
+                    ec[rows, cols] = e
+                    add = sublanes(e, jnp.add)
+                    total = add if total is None else total + add
+                cmax[part, q + g, :, cols] = peak
+                csum[part, q + g, :, cols] = total
 
     def tiles(first, last, strip):
         def body(q, carry):
@@ -274,7 +276,7 @@
     t2_recv()
     tile(3, 0, *LAST[0])
     c_come(2)
-    tiles(0, 3, 2)
+    tile(0, 2, *STRIPS[2], count=3)
     tile(3, 1, *LAST[1])
 
     for part in range(2):
@@ -448,7 +450,7 @@
         v = gi_mid[h]
         for a in range(1, 4):
             v = v + g2_in[h, a].astype(jnp.float32)
-        gi_out[pl.ds(32 * h, 32), :] = v
+        out[pl.ds(32 * h, 32), :] = v
 
     def scalar_send(level, peers, peer, me):
         for p in peers:
@@ -495,27 +497,28 @@
     text_parts(3)
     sc_snd[1] = scalar_sum(0, me_p)
     scalar_send(1, *in_column)
+    text_both(2)
+    chain_wait(1, 1)
+    chain_send(2, 1)
     for h in range(2):
         stage1_sum(h, 0)
-    text_both(2)
-    for second in (1, 0):
-        chain_wait(1, second)
-        chain_send(2, second)
+    chain_wait(1, 0)
+    chain_send(2, 0)
     for h in range(2):
         stage1_sum(h, 1)
     for h in range(2):
         stage1_sum(h, 2)
     text_both(3)
     total = scalar_sum(1, me_c)
+    for h in range(2):
+        stage2_sum(h)
     for second in (1, 0):
         chain_wait(2, second)
     for q in range(2):
-        gt_out[pl.ds(32 * q, 32), :] = own_part(0, q) + chain_part(1, 2, q) + chain_part(-1, 2, q)
-    for h in range(2):
-        stage2_sum(h)
+        out[pl.ds(ROWS + 32 * q, 32), :] = own_part(0, q) + chain_part(1, 2, q) + chain_part(-1, 2, q)
     pairs = 2.0 * TILE * 16
-    sums_out[pl.ds(0, 1), :] = total[:1] / pairs
-    sums_out[pl.ds(1, 1), :] = total[1:] / (pairs * sscale[0])
+    out[pl.ds(2 * ROWS, 1), pl.ds(0, 128)] = total[:1] / pairs
+    out[pl.ds(2 * ROWS + 1, 1), pl.ds(0, 128)] = total[1:] / (pairs * sscale[0])
     all_sent(img.at[pl.ds(0, 960)], ps_s, ps_r.at[0])
     all_sent(txt.at[pl.ds(0, 7), 0], zs_s, zs_r.at[0])
     all_sent(txt.at[:, 0], cs_s, cs_r.at[0])
@@ -528,11 +531,11 @@
     all_sent(sc_in.at[:, pl.ds(0, 15)], sc_s, sc_r.at[0])
 
 
-def finish(gi, gt, sums, gi_out, gt_out, loss_out, gs_out):
-    gi_out[...] = gi[...]
-    gt_out[...] = gt[...]
-    loss_out[0] = jnp.sum(sums[pl.ds(0, 1), :])
-    gs_out[0] = jnp.sum(sums[pl.ds(1, 1), :])
+def finish(both, gi_out, gt_out, loss_out, gs_out):
+    gi_out[...] = both[pl.ds(0, ROWS), :]
+    gt_out[...] = both[pl.ds(ROWS, ROWS), :]
+    loss_out[0] = jnp.sum(both[pl.ds(2 * ROWS, 1), pl.ds(0, 128)])
+    gs_out[0] = jnp.sum(both[pl.ds(2 * ROWS + 1, 1), pl.ds(0, 128)])
 
 
 def shards(*args):
@@ -544,11 +547,11 @@
     V = pltpu.VMEM
     rows = jax.ShapeDtypeStruct((ROWS, SW), f32)
     one = jax.ShapeDtypeStruct((1,), f32)
-    sums = pl.pallas_call(
+    results = pl.pallas_call(
         kernel,
-        out_shape=(rows, rows, jax.ShapeDtypeStruct((2, 128), f32)),
+        out_shape=jax.ShapeDtypeStruct((2 * ROWS + 8, SW), f32),
         in_specs=[anyw] * 4 + [smem] * 2,
-        out_specs=(vmem, vmem, vmem),
+        out_specs=vmem,
         scratch_shapes=[
             V((TILE, W), bf16),
             V((NZ, 2, ROWS, W), bf16),
@@ -601,9 +604,9 @@
     return tuple(pl.pallas_call(
         finish,
         out_shape=(rows, rows, one, one),
-        in_specs=[vmem] * 3,
+        in_specs=[vmem],
         out_specs=(vmem, vmem, smem, smem),
-    )(*sums))
+    )(results))
 
 
 def solution(mesh):

time: 60.8 us -> 59.7 us (0.982)
  Pallas kernels: 58.7 us -> 57.6 us
    pallas_call x2, Pallas kernels: 58.7 us -> 57.6 us  [the longest x1 55.9 us: shards(): pl.pallas_call(kernel, out_shape=jax.ShapeDtypeStruct((2 * ROWS + 8, SW),...]
where the time goes in v6:
time: 59.7 us; the launch traced here: 59.5 us
  Pallas kernels  57.6 us (96%)
  between operations  1.93 us (3%)
    pallas_call x1, Pallas kernels, shards(): pl.pallas_call(kernel, out_shape=jax.ShapeDtypeStruct((2 * ROWS + 8, SW),...  55.9 us
    pallas_call x1, Pallas kernels, shards(): pl.pallas_call(finish, out_shape=(rows, rows, one, one), in_specs=[vmem],...  1.68 us

profile of v6, /device:TPU:1, one launch (start us, length us, event | category | flops | bytes accessed | tf_op | source)
XLA Modules:
  0.0 59.5 jit_solution(17331339426302518368)
XLA Ops:
  1.9 55.9 %shard_map.93.both = f32[136,512]{1,0:T(8,128)} custom-call(bf16[64,1280]{1,0:T(8,128)(2,1)} %ti.1, bf16[64,1280]{1,0:T(8,128)(2,1)} %tt.1, bf16[64,512]{1,0:T(8,128)(2,1)} %si.1, bf16[64,512]{1,0:T(8,128)(2,1)} %st.1, f32[1]{0:T(128)S(6)} %copy.10.tscale, f32[1]{0:T(128)S(6)} %copy.11.sscale), custom_call_target="tpu_custom_call" | custom-call | tf_op jit(solution)/shard_map/pallas_call | solution.py:550
  57.8 1.7 %shard_map.94 = (f32[64,512]{1,0:T(8,128)}, f32[64,512]{1,0:T(8,128)}, f32[1]{0:T(128)}, f32[1]{0:T(128)}) custom-call(f32[136,512]{1,0:T(8,128)} %shard_map.93.both), custom_call_target="tpu_custom_call" | custom-call | tf_op jit(solution)/shard_map/pallas_call | solution.py:604

commit v7 on v6

--- a/solution.py
+++ b/solution.py
@@ -367,8 +367,8 @@
                 scale_acc = scale_acc + lanes(sublanes(differ * v, jnp.add), jnp.add)
             return loss_acc, scale_acc
 
-        carry = lax.fori_loop(0, 24, functools.partial(body, group=0), carry, unroll=2)
-        return lax.fori_loop(24, 32, functools.partial(body, group=1), carry, unroll=2)
+        carry = lax.fori_loop(0, 24, functools.partial(body, group=0), carry, unroll=4)
+        return lax.fori_loop(24, 32, functools.partial(body, group=1), carry, unroll=4)
 
     slots = ((5, 3), (3, 2), (1, 2), (0, 1))
 

time: 59.7 us -> 59.5 us (level)
  no operation moved by 1% of the time
where the time goes in v7:
time: 59.5 us; the launch traced here: 59.4 us
  Pallas kernels  57.4 us (96%)
  between operations  1.93 us (3%)
    pallas_call x1, Pallas kernels, shards(): pl.pallas_call(kernel, out_shape=jax.ShapeDtypeStruct((2 * ROWS + 8, SW),...  55.8 us
    pallas_call x1, Pallas kernels, shards(): pl.pallas_call(finish, out_shape=(rows, rows, one, one), in_specs=[vmem],...  1.68 us

profile of v7, /device:TPU:1, one launch (start us, length us, event | category | flops | bytes accessed | tf_op | source)
XLA Modules:
  0.0 59.4 jit_solution(9613410671996602593)
XLA Ops:
  1.9 55.8 %shard_map.93.both = f32[136,512]{1,0:T(8,128)} custom-call(bf16[64,1280]{1,0:T(8,128)(2,1)} %ti.1, bf16[64,1280]{1,0:T(8,128)(2,1)} %tt.1, bf16[64,512]{1,0:T(8,128)(2,1)} %si.1, bf16[64,512]{1,0:T(8,128)(2,1)} %st.1, f32[1]{0:T(128)S(6)} %copy.10.tscale, f32[1]{0:T(128)S(6)} %copy.11.sscale), custom_call_target="tpu_custom_call" | custom-call | tf_op jit(solution)/shard_map/pallas_call | solution.py:550
  57.7 1.7 %shard_map.94 = (f32[64,512]{1,0:T(8,128)}, f32[64,512]{1,0:T(8,128)}, f32[1]{0:T(128)}, f32[1]{0:T(128)}) custom-call(f32[136,512]{1,0:T(8,128)} %shard_map.93.both), custom_call_target="tpu_custom_call" | custom-call | tf_op jit(solution)/shard_map/pallas_call | solution.py:604
